TPU v7x, 256 devices: a whole 4x4x8 slice. The times are simulated.
256 devices in a mesh: lat: 16 (over y_hi, x, core), lon: 16 (over z, y_lo).
Axes of the slice: x: 4, y: 4 (y_hi: 2, y_lo: 2; y = y_hi * 2 + y_lo), z: 8, core: 2. Of those that a mesh axis runs over, the one named last changes fastest.
Arguments:
- tokens: bfloat16 [2, 96, 384, 512], P(None, 'lat', 'lon'), may hold values from -6 to 6
- cotangent: bfloat16 [2, 96, 384, 512], P(None, 'lat', 'lon'), may hold values from -6 to 6
- w_qkv: bfloat16 [512, 1536], replicated, may hold values from -6 to 6
- w_proj: bfloat16 [512, 512], replicated, may hold values from -0.25 to 0.25
- w_fc1: bfloat16 [512, 2048], replicated, may hold values from -0.25 to 0.25
- w_fc2: bfloat16 [2048, 512], replicated, may hold values from -0.125 to 0.125
Outputs:
- block_out: bfloat16 [2, 96, 384, 512], P(None, 'lat', 'lon')
- input_grad: bfloat16 [2, 96, 384, 512], P(None, 'lat', 'lon')
- weight_grads: float32 [24576, 128], P(('lat', 'lon'))
All inputs are finite; a program needn't handle non-finite values.
Results may differ from a plain program's by a relative error of at most 0.017.
Values may be sent and summed in bfloat16 or wider, within the bound.
A program may use at most 128 MiB of HBM per device.

v0:
```python
import jax
import jax.numpy as jnp
from jax import lax
from jax.experimental import pallas as pl
from jax.experimental.pallas import tpu as pltpu
from jax.sharding import PartitionSpec as P

MESH = pl.DeviceIdType.MESH
H = 16
D = 512
NT = 288
F32 = jnp.float32
BF16 = jnp.bfloat16

epsilon = 1e-05
neg_fill = -1e30
inv_root_two = 0.7071067811865476
inv_root_tau = 0.3989422804014327
grad_scale = 73728 ** (-0.5)


class Place:
    def __init__(self):
        lat, lon = lax.axis_index("lat"), lax.axis_index("lon")
        self.lat, self.lon = lat, lon
        self.core = lax.rem(lat, 2)
        self.x = lax.rem(lax.div(lat, 2), 4)
        self.y = lax.div(lat, 8) * 2 + lax.rem(lon, 2)
        self.z = lax.div(lon, 2)

    def shifted(self, axis=None, by=0):
        x, y, z, core = self.x, self.y, self.z, self.core
        if axis == "x":
            x = lax.rem(x + by, 4)
        elif axis == "y":
            y = lax.rem(y + by, 4)
        elif axis == "z":
            z = lax.rem(z + by, 8)
        elif axis == "core":
            core = 1 - core
        return (lax.div(y, 2) * 8 + x * 2 + core, z * 2 + lax.rem(y, 2))

    def neighbour(self, by_lat, by_lon):
        return (lax.rem(self.lat + by_lat, 16), lax.rem(self.lon + by_lon, 16))


SIZES = {"x": 4, "y": 4, "z": 8}
ORDERS = (("x", "y", "z"), ("y", "x", "z"), ("z", "x", "y"))


def row_order(place, order, own_core):
    p = lax.broadcasted_iota(jnp.int32, (256, 1), 0)
    r = p & 1
    rest = p >> 1
    off = {}
    for axis in reversed(order):
        bits = 3 if axis == "z" else 2
        off[axis] = rest & (SIZES[axis] - 1)
        rest = rest >> bits
    x = (off["x"] + place.x) & 3
    y = (off["y"] + place.y) & 3
    z = (off["z"] + place.z) & 7
    core = place.core if own_core else 1 - place.core
    row = ((((((y >> 1) * 4 + x) * 2 + core) * 8 + z) * 2 + (y & 1)) * 2) + r
    columns = lax.broadcasted_iota(jnp.int32, (256, D), 1)
    return jnp.where(columns == row, 1.0, 0.0).astype(BF16)


def dot(a, b, ca=1, cb=0):
    return lax.dot_general(a, b, (((ca,), (cb,)), ((), ())), preferred_element_type=F32)


class Copies:
    def __init__(self, send_sems, recv_sems):
        self.send_sems, self.recv_sems, self.used, self.started = send_sems, recv_sems, 0, []

    def send(self, src, dst, target):
        k = self.used
        self.used += 1
        copy = pltpu.make_async_remote_copy(
            src_ref=src,
            dst_ref=dst,
            send_sem=self.send_sems.at[k],
            recv_sem=self.recv_sems.at[k],
            device_id=target,
            device_id_type=MESH,
        )
        copy.start()
        self.started.append(copy)
        return copy

    def drain(self):
        for copy in self.started:
            copy.wait_send()


def add_into(acc, rows, cols, arrived, step=16):
    start, count = rows
    c0, cn = cols
    step = min(step, count)

    @pl.loop(0, count // step)
    def _(i):
        here = pl.ds(pl.multiple_of(start + i * step, step), step)
        there = pl.ds(pl.multiple_of(i * step, step), step)
        acc[here, c0 : c0 + cn] += arrived[there, :].astype(F32)


def cast_from(acc, rows, cols, out, step=16):
    start, count = rows
    c0, cn = cols
    step = min(step, count)

    @pl.loop(0, count // step)
    def _(i):
        here = pl.ds(pl.multiple_of(start + i * step, step), step)
        there = pl.ds(pl.multiple_of(i * step, step), step)
        out[there, :] = acc[here, c0 : c0 + cn].astype(BF16)


def sum_part(place, copies, part, width, bufs, acc, sent0, arrive0, emit):
    order = ORDERS[part]
    first, second, third = order
    n = SIZES[first]
    rows = 256 // n
    half = width // 2
    yield
    sent0.wait_recv()
    add_into(acc, (0, 256), (0, width), arrive0)
    ring_send, ring_recv = bufs["ring_send"], bufs["ring_recv"]
    for s in range(n // 2):
        kp, km = n // 2 - s, (n // 2 + s) % n
        if s == 0:
            plus_cols, minus_cols = (0, half), (half, half)
        else:
            plus_cols = minus_cols = (0, width)
        pend = []
        for way, chunk, cols, by in ((0, kp, plus_cols, 1), (1, km, minus_cols, n - 1)):
            span = (s * rows, rows)
            out = ring_send.at[way, pl.ds(s * rows, rows), pl.ds(0, cols[1])]
            inn = ring_recv.at[way, pl.ds(s * rows, rows), pl.ds(0, cols[1])]
            cast_from(acc, (chunk * rows, rows), cols, out)
            pend.append((copies.send(out, inn, place.shifted(first, by)), inn, cols))
        yield
        for way, (copy, inn, cols) in enumerate(pend):
            chunk = kp - 1 if way == 0 else (km + 1) % n
            copy.wait_recv()
            add_into(acc, (chunk * rows, rows), cols, inn)
    n2 = 4
    rows2 = rows // n2
    pend = []
    for j in range(1, n2):
        inn = bufs["mid_recv"].at[pl.ds((j - 1) * rows2, rows2)]
        if rows2 >= 16:
            out = bufs["mid_send"].at[pl.ds((j - 1) * rows2, rows2)]
            cast_from(acc, (j * rows2, rows2), (0, width), out)
        else:
            out = acc.at[pl.ds(j * rows2, rows2)]
        pend.append((copies.send(out, inn, place.shifted(second, j)), inn))
    yield
    total = acc[0:rows2, :]
    for copy, inn in pend:
        copy.wait_recv()
        total = total + inn[...].astype(F32)
    n3 = SIZES[third]
    tiles = width // 128
    last_send, last_recv = bufs["last_send"], bufs["last_recv"]
    for c in range(tiles):
        last_send[pl.ds(c, 2 * n3, stride=tiles), :] = total[:, c * 128 : (c + 1) * 128]
    pend = []
    for j in range(1, n3):
        out = last_send.at[pl.ds(j * 2 * tiles, 2 * tiles)]
        inn = last_recv.at[pl.ds((j - 1) * 2 * tiles, 2 * tiles)]
        pend.append((copies.send(out, inn, place.shifted(third, j)), inn))
    yield
    done = last_send[0 : 2 * tiles, :]
    for copy, inn in pend:
        copy.wait_recv()
        done = done + inn[...]
    done = done * grad_scale
    for r in range(2):
        for local, whole, count in emit:
            bufs["out"][r * 48 + whole : r * 48 + whole + count, :] = done[
                r * tiles + local : r * tiles + local + count, :
            ]


def part_scratch(width):
    out = []
    for order in ORDERS:
        n = SIZES[order[0]]
        rows = 256 // n
        n3 = SIZES[order[2]]
        tiles = width // 128
        wide = rows // 4 >= 16
        out.append(
            dict(
                ring_send=pltpu.VMEM((2, n // 2 * rows, width), BF16),
                ring_recv=pltpu.VMEM((2, n // 2 * rows, width), BF16),
                mid_send=pltpu.VMEM((3 * rows // 4, width), BF16) if wide else pltpu.VMEM((8, 128), F32),
                mid_recv=pltpu.VMEM((3 * rows // 4, width), BF16 if wide else F32),
                last_send=pltpu.VMEM((n3 * 2 * tiles, 128), F32),
                last_recv=pltpu.VMEM(((n3 - 1) * 2 * tiles, 128), F32),
            )
        )
    return out


def batch_scratch(width):
    return dict(
        send0=pltpu.VMEM((3, 256, width), BF16),
        recv0=pltpu.VMEM((3, 256, width), BF16),
        acc=pltpu.VMEM((3, 256, width), F32),
        parts=part_scratch(width),
    )


def greet(place):
    barrier = pltpu.get_barrier_semaphore()
    peers = [place.shifted("core")]
    for axis in ("x", "y", "z"):
        peers += [place.shifted(axis, by) for by in range(1, SIZES[axis])]
    for by in (1, 15):
        peers += [place.neighbour(by, 0), place.neighbour(0, by), place.neighbour(by, by)]
    for peer in peers:
        pl.semaphore_signal(barrier, inc=1, device_id=peer, device_id_type=MESH)
    pl.semaphore_wait(barrier, len(peers))


LATE = (
    (("qkv", 0, 512, 0),),
    (("qkv", 512, 512, 4),),
    (("qkv", 1024, 512, 8),),
)
EARLY = (
    (("fc1", 0, 1536, 16),),
    (("fc1", 1536, 512, 28), ("fc2", 0, 1024, 32)),
    (("fc2", 1024, 1024, 40), ("proj", 0, 512, 12)),
)


def start_batch(place, copies, split, width, scr, out_ref, pairs, orders_ref, lhs_ref):
    gens = []
    for part in range(3):
        acc = scr["acc"].at[part]
        send0 = scr["send0"].at[part]
        recv0 = scr["recv0"].at[part]
        for own in (0, 1):
            at = 0
            for name, begin, count, _ in split[part]:
                left, right = pairs[name]
                lhs_ref[...] = dot(orders_ref[2 * part + own], left[...], 1, 1).astype(BF16)
                base = at

                @pl.loop(0, count // 256)
                def _(i):
                    src = pl.ds(pl.multiple_of(begin + i * 256, 256), 256)
                    dst = pl.ds(pl.multiple_of(base + i * 256, 256), 256)
                    value = dot(lhs_ref[...], right[:, src])
                    if own:
                        acc[:, dst] = value
                    else:
                        send0[:, dst] = value.astype(BF16)

                at += count
            if not own:
                copy = copies.send(send0, recv0, place.shifted("core"))
        emit, at = [], 0
        for _, _, count, whole in split[part]:
            emit.append((at // 128, whole, count // 128))
            at += count
        bufs = dict(scr["parts"][part], out=out_ref)
        gens.append(sum_part(place, copies, part, width, bufs, acc, copy, recv0, emit))
    return gens


def tick(gens):
    left = []
    for gen in gens:
        try:
            next(gen)
            left.append(gen)
        except StopIteration:
            pass
    return left


PACKED = 320
SECTIONS = ((112, 112, 1, 0), (224, 48, 0, 1), (272, 48, 1, 1))


def token_of(s):
    big = s < 224
    second = ((s >= 112) & (s < 224)) | (s >= 272)
    u = jnp.where(big, s - jnp.where(s >= 112, 112, 0), s - jnp.where(s >= 272, 272, 224))
    low = jnp.where(second, 0, 3)
    wide = big & (u < 72)
    u2 = jnp.where(big, u - 72, u)
    lev_w = (u >= 36).astype(jnp.int32)
    m_w = u - 36 * lev_w
    row_w = (m_w >= 12).astype(jnp.int32) + (m_w >= 24).astype(jnp.int32)
    col_w = 6 + m_w - 12 * row_w
    lev_n = (u2 >= 18).astype(jnp.int32)
    m_n = u2 - 18 * lev_n
    row_n = (m_n >= 6).astype(jnp.int32) + (m_n >= 12).astype(jnp.int32)
    col_n = jnp.where(big, 18, 0) + m_n - 6 * row_n
    lev = jnp.where(wide, lev_w, lev_n)
    row = jnp.where(wide, row_w, row_n) + low
    col = jnp.where(wide, col_w, col_n)
    empty = u >= jnp.where(big, 108, 36)
    return jnp.where(empty, -1, lev * 144 + row * 24 + col)


def packed_of(w):
    at = jnp.where(w < 72, w, w + 40)
    at = jnp.where(w >= 144, w - 72, at)
    at = jnp.where(w >= 180, w + 44, at)
    at = jnp.where(w >= 216, w - 32, at)
    return jnp.where(w >= 252, w + 20, at)


def iota(shape, dim):
    return lax.broadcasted_iota(jnp.int32, shape, dim)


def ones_at(same):
    return jnp.where(same, 1.0, 0.0).astype(BF16)


def pack_matrix():
    return ones_at(token_of(iota((PACKED, 1), 0)) == iota((PACKED, NT), 1))


def unpack_matrix():
    return ones_at(token_of(iota((1, PACKED), 1)) == iota((NT, PACKED), 0))


def window_matrix():
    return ones_at(packed_of(iota((NT, 1), 0)) == iota((NT, PACKED), 1))


def unwindow_matrix():
    return ones_at(packed_of(iota((1, NT), 1)) == iota((PACKED, NT), 0))


def normalize(values):
    centre = values - jnp.mean(values, axis=-1, keepdims=True)
    inv_std = lax.rsqrt(jnp.mean(centre * centre, axis=-1, keepdims=True) + epsilon)
    return centre * inv_std, inv_std


def norm_back(upstream, normed, inv_std):
    mean_up = jnp.mean(upstream, axis=-1, keepdims=True)
    mean_dot = jnp.mean(upstream * normed, axis=-1, keepdims=True)
    return inv_std * (upstream - mean_up - normed * mean_dot)


def head_stack(value):
    lane = iota((144, 128), 1)
    zero = jnp.zeros_like(value)
    return jnp.concatenate([jnp.where((lane >> 5) == j, value, zero) for j in range(4)], axis=0)


def head_merge(value):
    lane = iota((144, 128), 1) >> 5
    out = value[432:576]
    for j in range(3):
        out = jnp.where(lane == j, value[144 * j : 144 * j + 144], out)
    return out


def block_kernel(
    x_ref, c_ref, wqkv_hbm, wproj_hbm, wfc1_hbm, wfc2_hbm,
    out_ref, gin_ref, wg_ref,
    early, late, orders_ref, lhs_ref, wqkv, wproj, wfc1, wfc2,
    packs, arrived, maps_p, maps_w, act_ref, gh_ref, qkv, gm, probs, bias, ctx, gctx, f32s, b16s, cols,
    send_sems, recv_sems, weight_sems,
):
    place = Place()
    copies = Copies(send_sems, recv_sems)
    loads = [
        pltpu.make_async_copy(src, dst, weight_sems.at[i])
        for i, (src, dst) in enumerate(((wqkv_hbm, wqkv), (wproj_hbm, wproj), (wfc1_hbm, wfc1), (wfc2_hbm, wfc2)))
    ]
    for load in loads:
        load.start()

    maps_p[0] = pack_matrix()
    greet(place)
    halos = []
    for i, ref in enumerate((x_ref, c_ref)):
        packs[i] = dot(maps_p[0], ref[...]).astype(BF16)
        halos.append(
            [
                copies.send(
                    packs.at[i, pl.ds(at, count)],
                    arrived.at[i, pl.ds(at, count)],
                    place.neighbour(16 - a if a else 0, 16 - b if b else 0),
                )
                for at, count, a, b in SECTIONS
            ]
        )
        arrived[i, 0:112] = packs[i, 0:112]
    maps_w[0] = window_matrix()
    maps_p[1] = unwindow_matrix()
    maps_w[1] = unpack_matrix()
    for part, order in enumerate(ORDERS):
        for own in (0, 1):
            orders_ref[2 * part + own] = row_order(place, order, own)
    last_band = place.lat == 15
    apart = ((iota((144, 144), 0) >= 72) != (iota((144, 144), 1) >= 72)) & last_band
    bias[...] = jnp.where(apart, neg_fill, 0.0)

    def return_home(slot, value):
        packs[slot] = dot(maps_p[1], value).astype(BF16)
        sent = [
            copies.send(
                packs.at[slot, pl.ds(at, count)],
                arrived.at[slot, pl.ds(at, count)],
                place.neighbour(a, b),
            )
            for at, count, a, b in SECTIONS
        ]
        arrived[slot, 0:112] = packs[slot, 0:112]
        return sent

    def arrive_home(slot, sent, ref):
        for copy in sent:
            copy.wait_recv()
        ref[...] = dot(maps_w[1], arrived[slot]).astype(BF16)

    X, N1, N2, G1 = 0, 1, 2, 3
    N1B, N2B, COT, GR = 0, 1, 2, 3
    R1, R2 = 0, 1

    for copy in halos[0]:
        copy.wait_recv()
    x = dot(maps_w[0], arrived[0])
    f32s[X] = x
    normed, inv_std = normalize(x)
    f32s[N1] = normed
    cols[R1] = inv_std
    b16s[N1B] = normed.astype(BF16)
    loads[0].wait()
    for i in range(3):
        part = dot(b16s[N1B], wqkv[:, 512 * i : 512 * i + 512])
        if i == 0:
            part = part * 32 ** (-0.5)
        qkv[:, 512 * i : 512 * i + 512] = part.astype(BF16)

    def group(i, which):
        w, g = lax.div(i, 4), lax.rem(i, 4)
        return pl.ds(pl.multiple_of(w * 144, 144), 144), pl.ds(pl.multiple_of(which * 512 + g * 128, 128), 128)

    @pl.loop(0, 8)
    def _(i):
        rows, lanes = group(i, 0)
        q = head_stack(qkv[rows, lanes])
        scores = dot(q, qkv[group(i, 1)], 1, 1)
        added = jnp.concatenate([bias[...]] * 4, axis=0)
        scores = scores + added
        raised = jnp.exp(scores - jnp.max(scores, axis=-1, keepdims=True))
        p = raised * (1.0 / jnp.sum(raised, axis=-1, keepdims=True))
        probs[i] = p
        ctx[rows, lanes] = head_merge(dot(p.astype(BF16), qkv[group(i, 2)])).astype(BF16)

    loads[1].wait()
    branch = dot(ctx[...], wproj[...]).astype(BF16)
    residual = (f32s[X] + branch.astype(F32)).astype(BF16)
    resid32 = residual.astype(F32)
    f32s[X] = resid32
    normed, inv_std = normalize(resid32)
    f32s[N2] = normed
    cols[R2] = inv_std
    b16s[N2B] = normed.astype(BF16)

    for copy in halos[1]:
        copy.wait_recv()
    b16s[COT] = dot(maps_w[0], arrived[1]).astype(BF16)
    loads[2].wait()
    loads[3].wait()

    @pl.loop(0, 8)
    def _(t):
        tile = pl.ds(pl.multiple_of(t * 256, 256), 256)
        hidden = dot(b16s[N2B], wfc1[:, tile])
        upper = 0.5 * (1.0 + lax.erf(hidden * inv_root_two))
        act_ref[:, tile] = (hidden * upper).astype(BF16)
        slope = upper + hidden * inv_root_tau * jnp.exp(-0.5 * hidden * hidden)
        gh_ref[:, tile] = (dot(b16s[COT], wfc2[tile, :], 1, 1) * slope).astype(BF16)

    grad_n2 = dot(gh_ref[...], wfc1[...], 1, 1)
    grad_resid = (b16s[COT].astype(F32) + norm_back(grad_n2, f32s[N2], cols[R2])).astype(BF16)
    b16s[GR] = grad_resid

    pairs = dict(
        qkv=(b16s.at[N1B], gm),
        proj=(ctx, b16s.at[GR]),
        fc1=(b16s.at[N2B], gh_ref),
        fc2=(b16s.at[COT], act_ref),
    )
    gens = start_batch(place, copies, EARLY, 1536, early, wg_ref, pairs, orders_ref, lhs_ref)

    block_out = (f32s[X] + dot(act_ref[...], wfc2[...])).astype(BF16)
    out_sent = return_home(2, block_out)
    gctx[...] = dot(b16s[GR], wproj[...], 1, 1).astype(BF16)

    for i in range(8):
        gens = tick(gens)
        w, g = i // 4, i % 4
        rows = slice(144 * w, 144 * w + 144)
        lanes = [slice(512 * j + 128 * g, 512 * j + 128 * g + 128) for j in range(3)]
        grad = head_stack(gctx[rows, lanes[0]])
        p = probs[i]
        grad_p = dot(grad, qkv[rows, lanes[2]], 1, 1)
        grad_s = (p * (grad_p - jnp.sum(grad_p * p, axis=-1, keepdims=True))).astype(BF16)
        gm[rows, lanes[2]] = dot(p.astype(BF16), grad, 0, 0).astype(BF16)
        gm[rows, lanes[0]] = (head_merge(dot(grad_s, qkv[rows, lanes[1]])) * 32 ** (-0.5)).astype(BF16)
        gm[rows, lanes[1]] = dot(grad_s, head_stack(qkv[rows, lanes[0]]), 0, 0).astype(BF16)

    gens += start_batch(place, copies, LATE, 512, late, wg_ref, pairs, orders_ref, lhs_ref)
    gens = tick(gens)
    grad_n1 = dot(gm[...], wqkv[...], 1, 1).astype(BF16).astype(F32)
    grad_in = b16s[GR].astype(F32) + norm_back(grad_n1, f32s[N1], cols[R1])
    in_sent = return_home(3, grad_in.astype(BF16))
    gens = tick(gens)
    arrive_home(2, out_sent, out_ref)
    gens = tick(gens)
    arrive_home(3, in_sent, gin_ref)
    while gens:
        gens = tick(gens)
    copies.drain()


def on_device(tokens, cotangent, w_qkv, w_proj, w_fc1, w_fc2):
    vmem = pl.BlockSpec(memory_space=pltpu.VMEM)
    hbm = pl.BlockSpec(memory_space=pl.ANY)
    out, gin, wg = pl.pallas_call(
        block_kernel,
        out_shape=(
            jax.ShapeDtypeStruct((NT, D), BF16),
            jax.ShapeDtypeStruct((NT, D), BF16),
            jax.ShapeDtypeStruct((96, 128), F32),
        ),
        in_specs=[vmem, vmem, hbm, hbm, hbm, hbm],
        out_specs=(vmem, vmem, vmem),
        scratch_shapes=[
            batch_scratch(1536),
            batch_scratch(512),
            pltpu.VMEM((6, 256, D), BF16),
            pltpu.VMEM((256, NT), BF16),
            pltpu.VMEM((D, 3 * D), BF16),
            pltpu.VMEM((D, D), BF16),
            pltpu.VMEM((D, 4 * D), BF16),
            pltpu.VMEM((4 * D, D), BF16),
            pltpu.VMEM((4, PACKED, D), BF16),
            pltpu.VMEM((4, PACKED, D), BF16),
            pltpu.VMEM((2, PACKED, NT), BF16),
            pltpu.VMEM((2, NT, PACKED), BF16),
            pltpu.VMEM((NT, 4 * D), BF16),
            pltpu.VMEM((NT, 4 * D), BF16),
            pltpu.VMEM((NT, 3 * D), BF16),
            pltpu.VMEM((NT, 3 * D), BF16),
            pltpu.VMEM((8, 576, 144), F32),
            pltpu.VMEM((144, 144), F32),
            pltpu.VMEM((NT, D), BF16),
            pltpu.VMEM((NT, D), BF16),
            pltpu.VMEM((3, NT, D), F32),
            pltpu.VMEM((4, NT, D), BF16),
            pltpu.VMEM((2, NT, 1), F32),
            pltpu.SemaphoreType.DMA((120,)),
            pltpu.SemaphoreType.DMA((120,)),
            pltpu.SemaphoreType.DMA((4,)),
        ],
        compiler_params=pltpu.CompilerParams(
            collective_id=0, has_side_effects=True, vmem_limit_bytes=60 * 1024 * 1024
        ),
    )(tokens.reshape(NT, D), cotangent.reshape(NT, D), w_qkv, w_proj, w_fc1, w_fc2)
    return out.reshape(tokens.shape), gin.reshape(tokens.shape), wg


def solution(mesh):
    return jax.shard_map(
        on_device,
        mesh=mesh,
        in_specs=(P(None, "lat", "lon", None), P(None, "lat", "lon", None), P(), P(), P(), P()),
        out_specs=(
            P(None, "lat", "lon", None),
            P(None, "lat", "lon", None),
            P(("lat", "lon"), None),
        ),
        check_vma=False,
    )
```

profile of v0, /device:TPU:8, one launch (start us, length us, event | category | flops | bytes accessed | tf_op | source)
XLA Modules:
  0.0 112.4 jit_solution(5752875173551829981)
XLA Ops:
  0.6 107.0 %shard_map.85 = (bf16[288,512]{1,0:T(8,128)(2,1)}, bf16[288,512]{1,0:T(8,128)(2,1)}, f32[96,128]{1,0:T(8,128)}) custom-call(bf16[288,512]{1,0:T(8,128)(2,1)} %bitcast.6, bf16[288,512]{1,0:T(8,128)(2,1)} %bitcast.7, bf16[512,1536]{1,0:T(8,128)(2,1)} %wqkv_hbm.1, bf16[512,512]{1,0:T(8,128)(2,1)} %wproj_hbm.1, bf16[512,2048]{1,0:T(8,128)(2,1)} %wfc1_hbm.1, ...), custom_call_target="tpu_custom_call" | custom-call | tf_op jit(solution)/shard_map/pallas_call | solution.py:538
  107.6 1.7 %copy.12 = bf16[2,6,24,512]{3,2,1,0:T(8,128)(2,1)} copy(bf16[2,6,24,512]{3,2,1,0:T(8,128)(2,1)} %bitcast.5) | data formatting | bytes 589824
  109.3 1.7 %copy.13 = bf16[2,6,24,512]{3,2,1,0:T(8,128)(2,1)} copy(bf16[2,6,24,512]{3,2,1,0:T(8,128)(2,1)} %bitcast.4) | data formatting | bytes 589824
  111.0 1.4 %copy.14 = f32[96,128]{1,0:T(8,128)} copy(f32[96,128]{1,0:T(8,128)} %get-tuple-element.14) | data formatting | bytes 98304
where the time goes:
time: 113 us; the launch traced here: 112 us
  Pallas kernels  107 us (95%)
  local copies, waits for them, and re-layouts  4.81 us (4%)
    pallas_call x1, Pallas kernels, on_device(): pl.pallas_call(block_kernel, out_shape=(jax.ShapeDtypeStruct((NT, D), BF1...  107 us
    unnamed x3, local copies, waits for them, and re-layouts  4.81 us

commit v1 on v0

v1 whole, which is shorter than its diff:
```python
import jax
import jax.numpy as jnp
from jax import lax
from jax.experimental import pallas as pl
from jax.experimental.pallas import tpu as pltpu
from jax.sharding import PartitionSpec as P

MESH = pl.DeviceIdType.MESH
H = 16
D = 512
NT = 288
F32 = jnp.float32
BF16 = jnp.bfloat16

epsilon = 1e-05
neg_fill = -1e30
inv_root_two = 0.7071067811865476
inv_root_tau = 0.3989422804014327
grad_scale = 73728 ** (-0.5)


class Place:
    def __init__(self):
        lat, lon = lax.axis_index("lat"), lax.axis_index("lon")
        self.lat, self.lon = lat, lon
        self.core = lax.rem(lat, 2)
        self.x = lax.rem(lax.div(lat, 2), 4)
        self.y = lax.div(lat, 8) * 2 + lax.rem(lon, 2)
        self.z = lax.div(lon, 2)

    def shifted(self, axis=None, by=0):
        x, y, z, core = self.x, self.y, self.z, self.core
        if axis == "x":
            x = lax.rem(x + by, 4)
        elif axis == "y":
            y = lax.rem(y + by, 4)
        elif axis == "z":
            z = lax.rem(z + by, 8)
        elif axis == "core":
            core = 1 - core
        return (lax.div(y, 2) * 8 + x * 2 + core, z * 2 + lax.rem(y, 2))

    def neighbour(self, by_lat, by_lon):
        return (lax.rem(self.lat + by_lat, 16), lax.rem(self.lon + by_lon, 16))


SIZES = {"x": 4, "y": 4, "z": 8}
ORDERS = (("x", "y", "z"), ("y", "x", "z"), ("z", "x", "y"))


def row_order(place, order):
    p = lax.broadcasted_iota(jnp.int32, (256, 1), 0)
    r = p & 1
    rest = p >> 1
    off = {}
    for axis in reversed(order):
        bits = 3 if axis == "z" else 2
        off[axis] = rest & (SIZES[axis] - 1)
        rest = rest >> bits
    x = (off["x"] + place.x) & 3
    y = (off["y"] + place.y) & 3
    z = (off["z"] + place.z) & 7
    row = ((((((y >> 1) * 4 + x) * 2 + place.core) * 8 + z) * 2 + (y & 1)) * 2) + r
    columns = lax.broadcasted_iota(jnp.int32, (256, D), 1)
    return jnp.where(columns == row, 1.0, 0.0).astype(BF16)


def dot(a, b, ca=1, cb=0):
    return lax.dot_general(a, b, (((ca,), (cb,)), ((), ())), preferred_element_type=F32)


class Copies:
    def __init__(self, send_sems, recv_sems):
        self.send_sems, self.recv_sems, self.used, self.started = send_sems, recv_sems, 0, []

    def send(self, src, dst, target):
        k = self.used
        self.used += 1
        copy = pltpu.make_async_remote_copy(
            src_ref=src,
            dst_ref=dst,
            send_sem=self.send_sems.at[k],
            recv_sem=self.recv_sems.at[k],
            device_id=target,
            device_id_type=MESH,
        )
        copy.start()
        self.started.append(copy)
        return copy

    def drain(self):
        for copy in self.started:
            copy.wait_send()


class Part:
    def __init__(self, place, copies, part, width, scr, emit, out_ref):
        self.place, self.copies, self.scr, self.width = place, copies, scr, width
        self.first, self.second, self.third = ORDERS[part]
        self.n1, self.n2, self.n3 = (SIZES[a] for a in ORDERS[part])
        self.rows1 = 256 // self.n1
        self.rows2 = self.rows1 // self.n2
        self.emit, self.out_ref = emit, out_ref
        self.pending = []

    def multiply(self, lhs, rhs, src, at, count):
        value = dot(lhs[...], rhs[:, src : src + count])
        self.scr["own"][:, at : at + count] = value[: self.rows1]
        self.scr["send1"][:, at : at + count] = value[self.rows1 :].astype(BF16)

    def send_first(self, at, count):
        r = self.rows1
        for j in range(1, self.n1):
            here = (pl.ds((j - 1) * r, r), pl.ds(at, count))
            self.pending.append(
                self.copies.send(
                    self.scr["send1"].at[here], self.scr["recv1"].at[here], self.place.shifted(self.first, j)
                )
            )

    def arrive(self):
        for copy in self.pending:
            copy.wait_recv()
        self.pending = []

    def second_step(self):
        self.arrive()
        scr, r1, r = self.scr, self.rows1, self.rows2
        whole = None
        if r < 16:
            whole = scr["own"][...]
            for i in range(self.n1 - 1):
                whole = whole + scr["recv1"][i * r1 : i * r1 + r1].astype(F32)
        for j in (2, 1, 3, 0):
            rows = slice(j * r, j * r + r)
            if r < 16:
                total = whole[rows]
            else:
                total = scr["own"][rows]
                for i in range(self.n1 - 1):
                    total = total + scr["recv1"][i * r1 + j * r : i * r1 + j * r + r].astype(F32)
            if j == 0:
                scr["own"][rows] = total
            else:
                here = pl.ds((j - 1) * r, r)
                scr["send2"][(j - 1) * r : j * r] = total.astype(scr["send2"].dtype)
                self.pending.append(
                    self.copies.send(
                        scr["send2"].at[here], scr["recv2"].at[here], self.place.shifted(self.second, j)
                    )
                )

    def third_step(self):
        self.arrive()
        scr, r = self.scr, self.rows2
        total = scr["own"][0:r]
        for i in range(self.n2 - 1):
            total = total + scr["recv2"][i * r : i * r + r].astype(F32)
        slots = scr["wide3"].shape[0] // (2 * self.n3)
        for c in range(self.width // 128):
            scr["wide3"][pl.ds(c, 2 * self.n3, stride=slots), :] = total[:, c * 128 : (c + 1) * 128]
        each = 2 * slots
        scr["send3"][...] = scr["wide3"][each:].astype(BF16)
        for j in range(1, self.n3):
            here = pl.ds((j - 1) * each, each)
            self.pending.append(
                self.copies.send(scr["send3"].at[here], scr["recv3"].at[here], self.place.shifted(self.third, j))
            )

    def finish(self):
        self.arrive()
        scr = self.scr
        slots = scr["wide3"].shape[0] // (2 * self.n3)
        each = 2 * slots
        total = scr["wide3"][0:each]
        for i in range(self.n3 - 1):
            total = total + scr["recv3"][i * each : (i + 1) * each].astype(F32)
        total = total * grad_scale
        for r in range(2):
            for local, whole, count in self.emit:
                self.out_ref[r * 48 + whole : r * 48 + whole + count, :] = total[
                    r * slots + local : r * slots + local + count, :
                ]


def part_scratch(part, width):
    n1, n2, n3 = (SIZES[a] for a in ORDERS[part])
    r1 = 256 // n1
    r2 = r1 // n2
    slots = -(-(width // 128) // 8) * 8
    mid = BF16 if r2 >= 16 else F32
    return dict(
        own=pltpu.VMEM((r1, width), F32),
        send1=pltpu.VMEM((256 - r1, width), BF16),
        recv1=pltpu.VMEM((256 - r1, width), BF16),
        send2=pltpu.VMEM((r1 - r2, width), mid),
        recv2=pltpu.VMEM((r1 - r2, width), mid),
        wide3=pltpu.VMEM((2 * n3 * slots, 128), F32),
        send3=pltpu.VMEM((2 * (n3 - 1) * slots, 128), BF16),
        recv3=pltpu.VMEM((2 * (n3 - 1) * slots, 128), BF16),
    )


EARLY = (2048, 2048, 512)
LATE = (640, 640, 256)
EARLY_OUT = (((0, 16, 16),), ((0, 32, 16),), ((0, 12, 4),))
LATE_OUT = (((0, 0, 4), (4, 8, 1)), ((0, 4, 4), (4, 9, 1)), ((0, 10, 2),))


def greet(place):
    barrier = pltpu.get_barrier_semaphore()
    peers = [place.shifted("core")]
    for axis in ("x", "y", "z"):
        peers += [place.shifted(axis, by) for by in range(1, SIZES[axis])]
    for by in (1, 15):
        peers += [place.neighbour(by, 0), place.neighbour(0, by), place.neighbour(by, by)]
    for peer in peers:
        pl.semaphore_signal(barrier, inc=1, device_id=peer, device_id_type=MESH)
    return lambda: pl.semaphore_wait(barrier, len(peers))


PACKED = 320
SECTIONS = ((112, 112, 1, 0), (224, 48, 0, 1), (272, 48, 1, 1))


def token_of(s):
    big = s < 224
    second = ((s >= 112) & (s < 224)) | (s >= 272)
    u = jnp.where(big, s - jnp.where(s >= 112, 112, 0), s - jnp.where(s >= 272, 272, 224))
    low = jnp.where(second, 0, 3)
    wide = big & (u < 72)
    u2 = jnp.where(big, u - 72, u)
    lev_w = (u >= 36).astype(jnp.int32)
    m_w = u - 36 * lev_w
    row_w = (m_w >= 12).astype(jnp.int32) + (m_w >= 24).astype(jnp.int32)
    col_w = 6 + m_w - 12 * row_w
    lev_n = (u2 >= 18).astype(jnp.int32)
    m_n = u2 - 18 * lev_n
    row_n = (m_n >= 6).astype(jnp.int32) + (m_n >= 12).astype(jnp.int32)
    col_n = jnp.where(big, 18, 0) + m_n - 6 * row_n
    lev = jnp.where(wide, lev_w, lev_n)
    row = jnp.where(wide, row_w, row_n) + low
    col = jnp.where(wide, col_w, col_n)
    empty = u >= jnp.where(big, 108, 36)
    return jnp.where(empty, -1, lev * 144 + row * 24 + col)


def packed_of(w):
    at = jnp.where(w < 72, w, w + 40)
    at = jnp.where(w >= 144, w - 72, at)
    at = jnp.where(w >= 180, w + 44, at)
    at = jnp.where(w >= 216, w - 32, at)
    return jnp.where(w >= 252, w + 20, at)


def iota(shape, dim):
    return lax.broadcasted_iota(jnp.int32, shape, dim)


def ones_at(same):
    return jnp.where(same, 1.0, 0.0).astype(BF16)


def pack_matrix():
    return ones_at(token_of(iota((PACKED, 1), 0)) == iota((PACKED, NT), 1))


def unpack_matrix():
    return ones_at(token_of(iota((1, PACKED), 1)) == iota((NT, PACKED), 0))


def window_matrix():
    return ones_at(packed_of(iota((NT, 1), 0)) == iota((NT, PACKED), 1))


def unwindow_matrix():
    return ones_at(packed_of(iota((1, NT), 1)) == iota((PACKED, NT), 0))


def normalize(values):
    centre = values - jnp.mean(values, axis=-1, keepdims=True)
    inv_std = lax.rsqrt(jnp.mean(centre * centre, axis=-1, keepdims=True) + epsilon)
    return centre * inv_std, inv_std


def norm_back(upstream, normed, inv_std):
    mean_up = jnp.mean(upstream, axis=-1, keepdims=True)
    mean_dot = jnp.mean(upstream * normed, axis=-1, keepdims=True)
    return inv_std * (upstream - mean_up - normed * mean_dot)


def head_stack(value):
    lane = iota((144, 128), 1)
    zero = jnp.zeros_like(value)
    return jnp.concatenate([jnp.where((lane >> 5) == j, value, zero) for j in range(4)], axis=0)


def head_merge(value):
    lane = iota((144, 128), 1) >> 5
    out = value[432:576]
    for j in range(3):
        out = jnp.where(lane == j, value[144 * j : 144 * j + 144], out)
    return out


OWN, SIB = slice(0, NT), slice(NT, 2 * NT)


def block_kernel(
    x_ref, c_ref, wqkv_hbm, wproj_hbm, wfc1_hbm, wfc2_hbm,
    out_ref, gin_ref, wg_ref,
    early, late, orders_ref, wqkv, wproj, wfc1, wfc2,
    packs, arrived, maps_p, maps_w, act, gh, n1b, n2b, cot, ctx, gr, gm,
    lhs_n1, lhs_n2, lhs_cot, lhs_ctx, qkv, probs, bias, gctx, f32s, cols,
    send_sems, recv_sems, weight_sems,
):
    place = Place()
    copies = Copies(send_sems, recv_sems)
    met = greet(place)
    loads = [
        pltpu.make_async_copy(src, dst, weight_sems.at[i])
        for i, (src, dst) in enumerate(((wqkv_hbm, wqkv), (wproj_hbm, wproj), (wfc1_hbm, wfc1), (wfc2_hbm, wfc2)))
    ]
    for load in loads:
        load.start()
    X, N1, N2 = 0, 1, 2
    R1, R2 = 0, 1

    def share(ref, at=0, count=None):
        here = pl.ds(at, ref.shape[1] if count is None else count)
        return copies.send(ref.at[pl.ds(0, NT), here], ref.at[pl.ds(NT, NT), here], place.shifted("core"))

    early = [
        Part(place, copies, i, width, scr, emit, wg_ref) for i, (width, scr, emit) in enumerate(zip(EARLY, early, EARLY_OUT))
    ]
    late = [
        Part(place, copies, i, width, scr, emit, wg_ref) for i, (width, scr, emit) in enumerate(zip(LATE, late, LATE_OUT))
    ]

    maps_p[0] = pack_matrix()
    packs[0] = dot(maps_p[0], x_ref[...]).astype(BF16)
    packs[1] = dot(maps_p[0], c_ref[...]).astype(BF16)
    maps_w[0] = window_matrix()
    maps_p[1] = unwindow_matrix()
    maps_w[1] = unpack_matrix()
    for part, order in enumerate(ORDERS):
        orders_ref[part] = row_order(place, order)
    apart = ((iota((144, 144), 0) >= 72) != (iota((144, 144), 1) >= 72)) & (place.lat == 15)
    bias[...] = jnp.where(apart, neg_fill, 0.0)
    met()
    halos = []
    for i in range(2):
        halos.append(
            [
                copies.send(
                    packs.at[i, pl.ds(at, count)],
                    arrived.at[i, pl.ds(at, count)],
                    place.neighbour(16 - a if a else 0, 16 - b if b else 0),
                )
                for at, count, a, b in SECTIONS
            ]
        )
        arrived[i, 0:112] = packs[i, 0:112]

    def return_home(slot, value):
        packs[slot] = dot(maps_p[1], value).astype(BF16)
        sent = [
            copies.send(
                packs.at[slot, pl.ds(at, count)],
                arrived.at[slot, pl.ds(at, count)],
                place.neighbour(a, b),
            )
            for at, count, a, b in SECTIONS
        ]
        arrived[slot, 0:112] = packs[slot, 0:112]
        return sent

    def arrive_home(slot, sent, ref):
        for copy in sent:
            copy.wait_recv()
        ref[...] = dot(maps_w[1], arrived[slot]).astype(BF16)

    for copy in halos[0]:
        copy.wait_recv()
    x = dot(maps_w[0], arrived[0])
    f32s[X] = x
    normed, inv_std = normalize(x)
    f32s[N1] = normed
    cols[R1] = inv_std
    n1b[OWN] = normed.astype(BF16)
    shared_n1 = share(n1b)
    loads[0].wait()
    for i in range(3):
        part = dot(n1b[OWN], wqkv[:, 512 * i : 512 * i + 512])
        if i == 0:
            part = part * 32 ** (-0.5)
        qkv[:, 512 * i : 512 * i + 512] = part.astype(BF16)

    def group(w, g):
        rows = slice(144 * w, 144 * w + 144)
        return rows, [slice(512 * j + 128 * g, 512 * j + 128 * g + 128) for j in range(3)]

    for w in range(2):
        for g in range(4):
            rows, (lq, lk, lv) = group(w, g)
            scores = dot(head_stack(qkv[rows, lq]), qkv[rows, lk], 1, 1)
            scores = scores + jnp.concatenate([bias[...]] * 4, axis=0)
            raised = jnp.exp(scores - jnp.max(scores, axis=-1, keepdims=True))
            p = raised * (1.0 / jnp.sum(raised, axis=-1, keepdims=True))
            probs[4 * w + g] = p
            ctx[rows, lq] = head_merge(dot(p.astype(BF16), qkv[rows, lv])).astype(BF16)

    shared_ctx = share(ctx)
    loads[1].wait()
    branch = dot(ctx[OWN], wproj[...]).astype(BF16)
    residual = (f32s[X] + branch.astype(F32)).astype(BF16)
    resid32 = residual.astype(F32)
    f32s[X] = resid32
    normed, inv_std = normalize(resid32)
    f32s[N2] = normed
    cols[R2] = inv_std
    n2b[OWN] = normed.astype(BF16)
    shared_n2 = share(n2b)

    for copy in halos[1]:
        copy.wait_recv()
    cot[OWN] = dot(maps_w[0], arrived[1]).astype(BF16)
    shared_cot = share(cot)
    loads[2].wait()
    loads[3].wait()
    shared_ff = []

    def forward_tile(t):
        tile = slice(512 * t, 512 * t + 512)
        hidden = dot(n2b[OWN], wfc1[:, tile])
        upper = 0.5 * (1.0 + lax.erf(hidden * inv_root_two))
        act[OWN, tile] = (hidden * upper).astype(BF16)
        slope = upper + hidden * inv_root_tau * jnp.exp(-0.5 * hidden * hidden)
        gh[OWN, tile] = (dot(cot[OWN], wfc2[tile, :], 1, 1) * slope).astype(BF16)
        shared_ff.append((share(act, 512 * t, 512), share(gh, 512 * t, 512)))

    def half(h):
        for pair in shared_ff[2 * h : 2 * h + 2]:
            for copy in pair:
                copy.wait_recv()
        for part, lhs, rhs in ((0, lhs_n2, gh), (1, lhs_cot, act)):
            early[part].multiply(lhs, rhs, 1024 * h, 1024 * h, 1024)
            early[part].send_first(1024 * h, 1024)

    for t in range(3):
        forward_tile(t)
    shared_n2.wait_recv()
    shared_cot.wait_recv()
    lhs_n2[...] = dot(orders_ref[0], n2b[...], 1, 1).astype(BF16)
    lhs_cot[...] = dot(orders_ref[1], cot[...], 1, 1).astype(BF16)
    half(0)
    forward_tile(3)
    grad_n2 = dot(gh[OWN], wfc1[...], 1, 1)
    grad_resid = (cot[OWN].astype(F32) + norm_back(grad_n2, f32s[N2], cols[R2])).astype(BF16)
    gr[OWN] = grad_resid
    shared_gr = share(gr)
    half(1)
    shared_ctx.wait_recv()
    lhs_ctx[...] = dot(orders_ref[2], ctx[...], 1, 1).astype(BF16)
    shared_gr.wait_recv()
    early[2].multiply(lhs_ctx, gr, 0, 0, 512)
    early[2].send_first(0, 512)

    block_out = (f32s[X] + dot(act[OWN], wfc2[...])).astype(BF16)
    out_sent = return_home(2, block_out)
    gctx[...] = dot(gr[OWN], wproj[...], 1, 1).astype(BF16)

    shared_n1.wait_recv()
    for i in range(3):
        lhs_n1[i] = dot(orders_ref[i], n1b[...], 1, 1).astype(BF16)
    shared_gm = []
    for g in range(4):
        for w in range(2):
            rows, (lq, lk, lv) = group(w, g)
            grad = head_stack(gctx[rows, lq])
            p = probs[4 * w + g]
            grad_p = dot(grad, qkv[rows, lv], 1, 1)
            grad_s = (p * (grad_p - jnp.sum(grad_p * p, axis=-1, keepdims=True))).astype(BF16)
            gm[rows, lv] = dot(p.astype(BF16), grad, 0, 0).astype(BF16)
            gm[rows, lq] = (head_merge(dot(grad_s, qkv[rows, lk])) * 32 ** (-0.5)).astype(BF16)
            gm[rows, lk] = dot(grad_s, head_stack(qkv[rows, lq]), 0, 0).astype(BF16)
        if g % 2:
            shared_gm += [share(gm, 512 * j + 128 * (g - 1), 256) for j in range(3)]

    for part in early:
        part.second_step()
    for copy in shared_gm:
        copy.wait_recv()
    for i in range(2):
        late[i].multiply(lhs_n1.at[i], gm, 512 * i, 0, 512)
        late[i].multiply(lhs_n1.at[i], gm, 1024 + 128 * i, 512, 128)
        late[i].send_first(0, 640)
    late[2].multiply(lhs_n1.at[2], gm, 1280, 0, 256)
    late[2].send_first(0, 256)
    grad_n1 = dot(gm[OWN], wqkv[...], 1, 1).astype(BF16).astype(F32)
    grad_in = gr[OWN].astype(F32) + norm_back(grad_n1, f32s[N1], cols[R1])
    in_sent = return_home(3, grad_in.astype(BF16))
    for part in early:
        part.third_step()
    for part in late:
        part.second_step()
    arrive_home(2, out_sent, out_ref)
    arrive_home(3, in_sent, gin_ref)
    for part in late:
        part.third_step()
    for part in early:
        part.finish()
    for part in late:
        part.finish()
    copies.drain()


def on_device(tokens, cotangent, w_qkv, w_proj, w_fc1, w_fc2):
    vmem = pl.BlockSpec(memory_space=pltpu.VMEM)
    hbm = pl.BlockSpec(memory_space=pl.ANY)
    both = 2 * NT
    out, gin, wg = pl.pallas_call(
        block_kernel,
        out_shape=(
            jax.ShapeDtypeStruct((NT, D), BF16),
            jax.ShapeDtypeStruct((NT, D), BF16),
            jax.ShapeDtypeStruct((96, 128), F32),
        ),
        in_specs=[vmem, vmem, hbm, hbm, hbm, hbm],
        out_specs=(vmem, vmem, vmem),
        scratch_shapes=[
            [part_scratch(i, w) for i, w in enumerate(EARLY)],
            [part_scratch(i, w) for i, w in enumerate(LATE)],
            pltpu.VMEM((3, 256, D), BF16),
            pltpu.VMEM((D, 3 * D), BF16),
            pltpu.VMEM((D, D), BF16),
            pltpu.VMEM((D, 4 * D), BF16),
            pltpu.VMEM((4 * D, D), BF16),
            pltpu.VMEM((4, PACKED, D), BF16),
            pltpu.VMEM((4, PACKED, D), BF16),
            pltpu.VMEM((2, PACKED, NT), BF16),
            pltpu.VMEM((2, NT, PACKED), BF16),
            pltpu.VMEM((both, 4 * D), BF16),
            pltpu.VMEM((both, 4 * D), BF16),
            pltpu.VMEM((both, D), BF16),
            pltpu.VMEM((both, D), BF16),
            pltpu.VMEM((both, D), BF16),
            pltpu.VMEM((both, D), BF16),
            pltpu.VMEM((both, D), BF16),
            pltpu.VMEM((both, 3 * D), BF16),
            pltpu.VMEM((3, 256, both), BF16),
            pltpu.VMEM((256, both), BF16),
            pltpu.VMEM((256, both), BF16),
            pltpu.VMEM((256, both), BF16),
            pltpu.VMEM((NT, 3 * D), BF16),
            pltpu.VMEM((8, 576, 144), F32),
            pltpu.VMEM((144, 144), F32),
            pltpu.VMEM((NT, D), BF16),
            pltpu.VMEM((3, NT, D), F32),
            pltpu.VMEM((2, NT, 1), F32),
            pltpu.SemaphoreType.DMA((120,)),
            pltpu.SemaphoreType.DMA((120,)),
            pltpu.SemaphoreType.DMA((4,)),
        ],
        compiler_params=pltpu.CompilerParams(
            collective_id=0, has_side_effects=True, vmem_limit_bytes=60 * 1024 * 1024
        ),
    )(tokens.reshape(NT, D), cotangent.reshape(NT, D), w_qkv, w_proj, w_fc1, w_fc2)
    return out.reshape(tokens.shape), gin.reshape(tokens.shape), wg


def solution(mesh):
    return jax.shard_map(
        on_device,
        mesh=mesh,
        in_specs=(P(None, "lat", "lon", None), P(None, "lat", "lon", None), P(), P(), P(), P()),
        out_specs=(
            P(None, "lat", "lon", None),
            P(None, "lat", "lon", None),
            P(("lat", "lon"), None),
        ),
        check_vma=False,
    )
```

time: 113 us -> 66.4 us (0.59)
  Pallas kernels: 107 us -> 59.8 us
    pallas_call x1, Pallas kernels: 107 us -> 59.8 us  [on_device(): pl.pallas_call(block_kernel, out_shape=(jax.ShapeDtypeStruct((NT, D), BF1...]
where the time goes in v1:
time: 66.4 us; the launch traced here: 65.2 us
  Pallas kernels  59.8 us (90%)
  local copies, waits for them, and re-layouts  4.81 us (7%)
    pallas_call x1, Pallas kernels, on_device(): pl.pallas_call(block_kernel, out_shape=(jax.ShapeDtypeStruct((NT, D), BF1...  59.8 us
    unnamed x3, local copies, waits for them, and re-layouts  4.81 us

profile of v1, /device:TPU:8, one launch (start us, length us, event | category | flops | bytes accessed | tf_op | source)
XLA Modules:
  0.0 65.2 jit_solution(17690897944080953884)
XLA Ops:
  0.6 59.8 %shard_map.85 = (bf16[288,512]{1,0:T(8,128)(2,1)}, bf16[288,512]{1,0:T(8,128)(2,1)}, f32[96,128]{1,0:T(8,128)}) custom-call(bf16[288,512]{1,0:T(8,128)(2,1)} %bitcast.6, bf16[288,512]{1,0:T(8,128)(2,1)} %bitcast.7, bf16[512,1536]{1,0:T(8,128)(2,1)} %wqkv_hbm.1, bf16[512,512]{1,0:T(8,128)(2,1)} %wproj_hbm.1, bf16[512,2048]{1,0:T(8,128)(2,1)} %wfc1_hbm.1, ...), custom_call_target="tpu_custom_call" | custom-call | tf_op jit(solution)/shard_map/pallas_call | solution.py:522
  60.4 1.7 %copy.12 = bf16[2,6,24,512]{3,2,1,0:T(8,128)(2,1)} copy(bf16[2,6,24,512]{3,2,1,0:T(8,128)(2,1)} %bitcast.5) | data formatting | bytes 589824
  62.1 1.7 %copy.13 = bf16[2,6,24,512]{3,2,1,0:T(8,128)(2,1)} copy(bf16[2,6,24,512]{3,2,1,0:T(8,128)(2,1)} %bitcast.4) | data formatting | bytes 589824
  63.8 1.4 %copy.14 = f32[96,128]{1,0:T(8,128)} copy(f32[96,128]{1,0:T(8,128)} %get-tuple-element.14) | data formatting | bytes 98304

commit v2 on v1

--- a/solution.py
+++ b/solution.py
@@ -202,9 +202,9 @@
 
 
 EARLY = (2048, 2048, 512)
-LATE = (640, 640, 256)
+LATE = (768, 768)
 EARLY_OUT = (((0, 16, 16),), ((0, 32, 16),), ((0, 12, 4),))
-LATE_OUT = (((0, 0, 4), (4, 8, 1)), ((0, 4, 4), (4, 9, 1)), ((0, 10, 2),))
+LATE_OUT = (((0, 0, 2), (2, 8, 1), (3, 2, 2), (5, 10, 1)), ((0, 4, 2), (2, 9, 1), (3, 6, 2), (5, 11, 1)))
 
 
 def greet(place):
@@ -439,40 +439,50 @@
         gh[OWN, tile] = (dot(cot[OWN], wfc2[tile, :], 1, 1) * slope).astype(BF16)
         shared_ff.append((share(act, 512 * t, 512), share(gh, 512 * t, 512)))
 
-    def half(h):
-        for pair in shared_ff[2 * h : 2 * h + 2]:
-            for copy in pair:
-                copy.wait_recv()
+    def quarter(t):
+        for copy in shared_ff[t]:
+            copy.wait_recv()
         for part, lhs, rhs in ((0, lhs_n2, gh), (1, lhs_cot, act)):
-            early[part].multiply(lhs, rhs, 1024 * h, 1024 * h, 1024)
-            early[part].send_first(1024 * h, 1024)
-
-    for t in range(3):
-        forward_tile(t)
+            early[part].multiply(lhs, rhs, 512 * t, 512 * t, 512)
+            early[part].send_first(512 * t, 512)
+
+    forward_tile(0)
+    forward_tile(1)
     shared_n2.wait_recv()
     shared_cot.wait_recv()
     lhs_n2[...] = dot(orders_ref[0], n2b[...], 1, 1).astype(BF16)
     lhs_cot[...] = dot(orders_ref[1], cot[...], 1, 1).astype(BF16)
-    half(0)
+    quarter(0)
+    forward_tile(2)
+    quarter(1)
     forward_tile(3)
+    quarter(2)
     grad_n2 = dot(gh[OWN], wfc1[...], 1, 1)
     grad_resid = (cot[OWN].astype(F32) + norm_back(grad_n2, f32s[N2], cols[R2])).astype(BF16)
     gr[OWN] = grad_resid
     shared_gr = share(gr)
-    half(1)
+    quarter(3)
+    block_out = (f32s[X] + dot(act[OWN], wfc2[...])).astype(BF16)
+    out_sent = return_home(2, block_out)
+    gctx[...] = dot(gr[OWN], wproj[...], 1, 1).astype(BF16)
     shared_ctx.wait_recv()
     lhs_ctx[...] = dot(orders_ref[2], ctx[...], 1, 1).astype(BF16)
     shared_gr.wait_recv()
     early[2].multiply(lhs_ctx, gr, 0, 0, 512)
     early[2].send_first(0, 512)
 
-    block_out = (f32s[X] + dot(act[OWN], wfc2[...])).astype(BF16)
-    out_sent = return_home(2, block_out)
-    gctx[...] = dot(gr[OWN], wproj[...], 1, 1).astype(BF16)
-
     shared_n1.wait_recv()
-    for i in range(3):
+    for i in range(2):
         lhs_n1[i] = dot(orders_ref[i], n1b[...], 1, 1).astype(BF16)
+
+    def late_half(h, shared):
+        for copy in shared:
+            copy.wait_recv()
+        for i in range(2):
+            late[i].multiply(lhs_n1.at[i], gm, 512 * i + 256 * h, 384 * h, 256)
+            late[i].multiply(lhs_n1.at[i], gm, 1024 + 256 * h + 128 * i, 384 * h + 256, 128)
+            late[i].send_first(384 * h, 384)
+
     shared_gm = []
     for g in range(4):
         for w in range(2):
@@ -484,27 +494,24 @@
             gm[rows, lv] = dot(p.astype(BF16), grad, 0, 0).astype(BF16)
             gm[rows, lq] = (head_merge(dot(grad_s, qkv[rows, lk])) * 32 ** (-0.5)).astype(BF16)
             gm[rows, lk] = dot(grad_s, head_stack(qkv[rows, lq]), 0, 0).astype(BF16)
-        if g % 2:
-            shared_gm += [share(gm, 512 * j + 128 * (g - 1), 256) for j in range(3)]
-
+        if g == 1:
+            shared_gm.append([share(gm, 512 * j, 256) for j in range(3)])
+        if g == 2:
+            late_half(0, shared_gm[0])
+        if g >= 2:
+            shared_gm.append([share(gm, 512 * j + 128 * g, 128) for j in range(3)])
+
+    grad_n1 = dot(gm[OWN], wqkv[...], 1, 1).astype(BF16)
+    late_half(1, shared_gm[1] + shared_gm[2])
     for part in early:
         part.second_step()
-    for copy in shared_gm:
-        copy.wait_recv()
-    for i in range(2):
-        late[i].multiply(lhs_n1.at[i], gm, 512 * i, 0, 512)
-        late[i].multiply(lhs_n1.at[i], gm, 1024 + 128 * i, 512, 128)
-        late[i].send_first(0, 640)
-    late[2].multiply(lhs_n1.at[2], gm, 1280, 0, 256)
-    late[2].send_first(0, 256)
-    grad_n1 = dot(gm[OWN], wqkv[...], 1, 1).astype(BF16).astype(F32)
-    grad_in = gr[OWN].astype(F32) + norm_back(grad_n1, f32s[N1], cols[R1])
+    grad_in = gr[OWN].astype(F32) + norm_back(grad_n1.astype(F32), f32s[N1], cols[R1])
     in_sent = return_home(3, grad_in.astype(BF16))
+    arrive_home(2, out_sent, out_ref)
+    for part in late:
+        part.second_step()
     for part in early:
         part.third_step()
-    for part in late:
-        part.second_step()
-    arrive_home(2, out_sent, out_ref)
     arrive_home(3, in_sent, gin_ref)
     for part in late:
         part.third_step()
@@ -558,8 +565,8 @@
             pltpu.VMEM((NT, D), BF16),
             pltpu.VMEM((3, NT, D), F32),
             pltpu.VMEM((2, NT, 1), F32),
-            pltpu.SemaphoreType.DMA((120,)),
-            pltpu.SemaphoreType.DMA((120,)),
+            pltpu.SemaphoreType.DMA((128,)),
+            pltpu.SemaphoreType.DMA((128,)),
             pltpu.SemaphoreType.DMA((4,)),
         ],
         compiler_params=pltpu.CompilerParams(

time: 66.4 us -> 64.2 us (0.967); the launches traced: 65.2 us -> 63.9 us
  Pallas kernels: 59.8 us -> 58.5 us
    pallas_call x1, Pallas kernels: 59.8 us -> 58.5 us  [on_device(): pl.pallas_call(block_kernel, out_shape=(jax.ShapeDtypeStruct((NT, D), BF1...]
where the time goes in v2:
time: 64.2 us; the launch traced here: 63.9 us
  Pallas kernels  58.5 us (91%)
  local copies, waits for them, and re-layouts  4.81 us (7%)
    pallas_call x1, Pallas kernels, on_device(): pl.pallas_call(block_kernel, out_shape=(jax.ShapeDtypeStruct((NT, D), BF1...  58.5 us
    unnamed x3, local copies, waits for them, and re-layouts  4.81 us

profile of v2, /device:TPU:8, one launch (start us, length us, event | category | flops | bytes accessed | tf_op | source)
XLA Modules:
  0.0 63.9 jit_solution(2536113452167200956)
XLA Ops:
  0.6 58.5 %shard_map.85 = (bf16[288,512]{1,0:T(8,128)(2,1)}, bf16[288,512]{1,0:T(8,128)(2,1)}, f32[96,128]{1,0:T(8,128)}) custom-call(bf16[288,512]{1,0:T(8,128)(2,1)} %bitcast.6, bf16[288,512]{1,0:T(8,128)(2,1)} %bitcast.7, bf16[512,1536]{1,0:T(8,128)(2,1)} %wqkv_hbm.1, bf16[512,512]{1,0:T(8,128)(2,1)} %wproj_hbm.1, bf16[512,2048]{1,0:T(8,128)(2,1)} %wfc1_hbm.1, ...), custom_call_target="tpu_custom_call" | custom-call | tf_op jit(solution)/shard_map/pallas_call | solution.py:529
  59.1 1.7 %copy.12 = bf16[2,6,24,512]{3,2,1,0:T(8,128)(2,1)} copy(bf16[2,6,24,512]{3,2,1,0:T(8,128)(2,1)} %bitcast.5) | data formatting | bytes 589824
  60.8 1.7 %copy.13 = bf16[2,6,24,512]{3,2,1,0:T(8,128)(2,1)} copy(bf16[2,6,24,512]{3,2,1,0:T(8,128)(2,1)} %bitcast.4) | data formatting | bytes 589824
  62.5 1.4 %copy.14 = f32[96,128]{1,0:T(8,128)} copy(f32[96,128]{1,0:T(8,128)} %get-tuple-element.14) | data formatting | bytes 98304

commit v3 on v2

--- a/solution.py
+++ b/solution.py
@@ -87,6 +87,10 @@
         copy.start()
         self.started.append(copy)
         return copy
+
+    def left(self, copy):
+        copy.wait_send()
+        self.started.remove(copy)
 
     def drain(self):
         for copy in self.started:
@@ -307,19 +311,28 @@
 
 
 def block_kernel(
-    x_ref, c_ref, wqkv_hbm, wproj_hbm, wfc1_hbm, wfc2_hbm,
-    out_ref, gin_ref, wg_ref,
+    x_hbm, c_hbm, wqkv_hbm, wproj_hbm, wfc1_hbm, wfc2_hbm,
+    out_hbm, gin_hbm, wg_ref,
     early, late, orders_ref, wqkv, wproj, wfc1, wfc2,
     packs, arrived, maps_p, maps_w, act, gh, n1b, n2b, cot, ctx, gr, gm,
-    lhs_n1, lhs_n2, lhs_cot, lhs_ctx, qkv, probs, bias, gctx, f32s, cols,
-    send_sems, recv_sems, weight_sems,
+    lhs_n1, lhs_n2, lhs_cot, lhs_ctx, qkv, probs, bias, gctx, f32s, cols, ends,
+    send_sems, recv_sems, local_sems,
 ):
     place = Place()
     copies = Copies(send_sems, recv_sems)
     met = greet(place)
     loads = [
-        pltpu.make_async_copy(src, dst, weight_sems.at[i])
-        for i, (src, dst) in enumerate(((wqkv_hbm, wqkv), (wproj_hbm, wproj), (wfc1_hbm, wfc1), (wfc2_hbm, wfc2)))
+        pltpu.make_async_copy(src, dst, local_sems.at[i])
+        for i, (src, dst) in enumerate(
+            (
+                (x_hbm, ends.at[0]),
+                (c_hbm, ends.at[1]),
+                (wqkv_hbm, wqkv),
+                (wproj_hbm, wproj),
+                (wfc1_hbm, wfc1),
+                (wfc2_hbm, wfc2),
+            )
+        )
     ]
     for load in loads:
         load.start()
@@ -338,8 +351,9 @@
     ]
 
     maps_p[0] = pack_matrix()
-    packs[0] = dot(maps_p[0], x_ref[...]).astype(BF16)
-    packs[1] = dot(maps_p[0], c_ref[...]).astype(BF16)
+    for i in range(2):
+        loads[i].wait()
+        packs[i] = dot(maps_p[0], ends[i]).astype(BF16)
     maps_w[0] = window_matrix()
     maps_p[1] = unwindow_matrix()
     maps_w[1] = unpack_matrix()
@@ -350,6 +364,9 @@
     met()
     halos = []
     for i in range(2):
+        if i:
+            for copy in halos[0]:
+                copies.left(copy)
         halos.append(
             [
                 copies.send(
@@ -378,7 +395,10 @@
     def arrive_home(slot, sent, ref):
         for copy in sent:
             copy.wait_recv()
-        ref[...] = dot(maps_w[1], arrived[slot]).astype(BF16)
+        ends[slot] = dot(maps_w[1], arrived[slot]).astype(BF16)
+        store = pltpu.make_async_copy(ends.at[slot], ref, local_sems.at[4 + slot])
+        store.start()
+        return store
 
     for copy in halos[0]:
         copy.wait_recv()
@@ -389,7 +409,7 @@
     cols[R1] = inv_std
     n1b[OWN] = normed.astype(BF16)
     shared_n1 = share(n1b)
-    loads[0].wait()
+    loads[2].wait()
     for i in range(3):
         part = dot(n1b[OWN], wqkv[:, 512 * i : 512 * i + 512])
         if i == 0:
@@ -411,7 +431,7 @@
             ctx[rows, lq] = head_merge(dot(p.astype(BF16), qkv[rows, lv])).astype(BF16)
 
     shared_ctx = share(ctx)
-    loads[1].wait()
+    loads[3].wait()
     branch = dot(ctx[OWN], wproj[...]).astype(BF16)
     residual = (f32s[X] + branch.astype(F32)).astype(BF16)
     resid32 = residual.astype(F32)
@@ -426,8 +446,8 @@
         copy.wait_recv()
     cot[OWN] = dot(maps_w[0], arrived[1]).astype(BF16)
     shared_cot = share(cot)
-    loads[2].wait()
-    loads[3].wait()
+    loads[4].wait()
+    loads[5].wait()
     shared_ff = []
 
     def forward_tile(t):
@@ -507,19 +527,27 @@
         part.second_step()
     grad_in = gr[OWN].astype(F32) + norm_back(grad_n1.astype(F32), f32s[N1], cols[R1])
     in_sent = return_home(3, grad_in.astype(BF16))
-    arrive_home(2, out_sent, out_ref)
+    out_stored = arrive_home(2, out_sent, out_hbm)
     for part in late:
         part.second_step()
     for part in early:
         part.third_step()
-    arrive_home(3, in_sent, gin_ref)
+    gin_stored = arrive_home(3, in_sent, gin_hbm)
     for part in late:
         part.third_step()
     for part in early:
         part.finish()
     for part in late:
         part.finish()
+    out_stored.wait()
+    gin_stored.wait()
     copies.drain()
+
+
+def hand_over(*refs):
+    count = len(refs) // 2
+    for i in range(count):
+        refs[count + i][...] = refs[i][...]
 
 
 def on_device(tokens, cotangent, w_qkv, w_proj, w_fc1, w_fc2):
@@ -533,8 +561,8 @@
             jax.ShapeDtypeStruct((NT, D), BF16),
             jax.ShapeDtypeStruct((96, 128), F32),
         ),
-        in_specs=[vmem, vmem, hbm, hbm, hbm, hbm],
-        out_specs=(vmem, vmem, vmem),
+        in_specs=[hbm] * 6,
+        out_specs=(hbm, hbm, vmem),
         scratch_shapes=[
             [part_scratch(i, w) for i, w in enumerate(EARLY)],
             [part_scratch(i, w) for i, w in enumerate(LATE)],
@@ -565,14 +593,21 @@
             pltpu.VMEM((NT, D), BF16),
             pltpu.VMEM((3, NT, D), F32),
             pltpu.VMEM((2, NT, 1), F32),
+            pltpu.VMEM((4, NT, D), BF16),
             pltpu.SemaphoreType.DMA((128,)),
             pltpu.SemaphoreType.DMA((128,)),
-            pltpu.SemaphoreType.DMA((4,)),
+            pltpu.SemaphoreType.DMA((8,)),
         ],
         compiler_params=pltpu.CompilerParams(
             collective_id=0, has_side_effects=True, vmem_limit_bytes=60 * 1024 * 1024
         ),
     )(tokens.reshape(NT, D), cotangent.reshape(NT, D), w_qkv, w_proj, w_fc1, w_fc2)
+    out, gin, wg = pl.pallas_call(
+        hand_over,
+        out_shape=tuple(jax.ShapeDtypeStruct(v.shape, v.dtype) for v in (out, gin, wg)),
+        in_specs=[vmem] * 3,
+        out_specs=(vmem,) * 3,
+    )(out, gin, wg)
     return out.reshape(tokens.shape), gin.reshape(tokens.shape), wg
 
 

time: 64.2 us -> 60.2 us (0.938)
  local copies, waits for them, and re-layouts: 4.81 us -> 0 us
  Pallas kernels: 58.5 us -> 59.5 us
    unnamed x3 -> x0, local copies, waits for them, and re-layouts: 4.81 us -> none
    pallas_call x0 -> x1, Pallas kernels: none -> 1.89 us  [on_device(): pl.pallas_call(hand_over, out_shape=tuple((jax.ShapeDtypeStruct(v.shape,...]
    pallas_call x1, Pallas kernels: 58.5 us -> 57.6 us  [on_device(): pl.pallas_call(block_kernel, out_shape=(jax.ShapeDtypeStruct((NT, D), BF1...]
where the time goes in v3:
time: 60.2 us; the launch traced here: 60.1 us
  Pallas kernels  59.5 us (99%)
  between operations  0.64 us (1%)
    pallas_call x1, Pallas kernels, on_device(): pl.pallas_call(block_kernel, out_shape=(jax.ShapeDtypeStruct((NT, D), BF1...  57.6 us
    pallas_call x1, Pallas kernels, on_device(): pl.pallas_call(hand_over, out_shape=tuple((jax.ShapeDtypeStruct(v.shape,...  1.89 us

profile of v3, /device:TPU:8, one launch (start us, length us, event | category | flops | bytes accessed | tf_op | source)
XLA Modules:
  0.0 60.1 jit_solution(1058066744798248495)
XLA Ops:
  0.6 57.6 %shard_map.85 = (bf16[288,512]{1,0:T(8,128)(2,1)}, bf16[288,512]{1,0:T(8,128)(2,1)}, f32[96,128]{1,0:T(8,128)}) custom-call(bf16[288,512]{1,0:T(8,128)(2,1)} %bitcast.4, bf16[288,512]{1,0:T(8,128)(2,1)} %bitcast.5, bf16[512,1536]{1,0:T(8,128)(2,1)} %wqkv_hbm.1, bf16[512,512]{1,0:T(8,128)(2,1)} %wproj_hbm.1, bf16[512,2048]{1,0:T(8,128)(2,1)} %wfc1_hbm.1, ...), custom_call_target="tpu_custom_call" | custom-call | tf_op jit(solution)/shard_map/pallas_call | solution.py:557
  58.2 1.9 %shard_map.86 = (bf16[288,512]{1,0:T(8,128)(2,1)}, bf16[288,512]{1,0:T(8,128)(2,1)}, f32[96,128]{1,0:T(8,128)}) custom-call(bf16[288,512]{1,0:T(8,128)(2,1)} %get-tuple-element.9.refs_0_, bf16[288,512]{1,0:T(8,128)(2,1)} %get-tuple-element.10.refs_1_, f32[96,128]{1,0:T(8,128)} %get-tuple-element.11.refs_2_), custom_call_target="tpu_custom_call" | custom-call | tf_op jit(solution)/shard_map/pallas_call | solution.py:605

commit v4 on v3

--- a/solution.py
+++ b/solution.py
@@ -105,14 +105,37 @@
         self.rows1 = 256 // self.n1
         self.rows2 = self.rows1 // self.n2
         self.emit, self.out_ref = emit, out_ref
-        self.pending = []
+        self.pending, self.relays, self.spans = [], [], []
 
     def multiply(self, lhs, rhs, src, at, count):
         value = dot(lhs[...], rhs[:, src : src + count])
         self.scr["own"][:, at : at + count] = value[: self.rows1]
         self.scr["send1"][:, at : at + count] = value[self.rows1 :].astype(BF16)
 
+    def send_ring(self, at, count):
+        r, half = self.rows1, count // 2
+        lo, hi, kept = pl.ds(at, half), pl.ds(at + half, half), pl.ds(at // 2, half)
+        plus, minus = self.place.shifted(self.first, 1), self.place.shifted(self.first, 3)
+        near, opposite, far = pl.ds(0, r), pl.ds(r, r), pl.ds(2 * r, r)
+        out, into, relay = self.scr["send1"], self.scr["recv1"], self.scr["relay"]
+        first = self.copies.send(out.at[opposite, lo], relay.at[near, kept], plus)
+        second = self.copies.send(out.at[opposite, hi], relay.at[opposite, kept], minus)
+        self.pending.append(self.copies.send(out.at[near, hi], into.at[near, hi], plus))
+        self.pending.append(self.copies.send(out.at[far, lo], into.at[far, lo], minus))
+        self.relays.append((first, (near, lo, near, kept), plus))
+        self.relays.append((second, (far, hi, opposite, kept), minus))
+        self.spans.append((at, count, (0, 2)))
+
+    def relay(self):
+        out, into, relay = self.scr["send1"], self.scr["recv1"], self.scr["relay"]
+        for copy, (rows, span, from_rows, kept), target in self.relays[:2]:
+            copy.wait_recv()
+            out[rows, span] = (out[rows, span].astype(F32) + relay[from_rows, kept].astype(F32)).astype(BF16)
+            self.pending.append(self.copies.send(out.at[rows, span], into.at[rows, span], target))
+        self.relays = self.relays[2:]
+
     def send_first(self, at, count):
+        self.spans.append((at, count, range(self.n1 - 1)))
         r = self.rows1
         for j in range(1, self.n1):
             here = (pl.ds((j - 1) * r, r), pl.ds(at, count))
@@ -130,29 +153,30 @@
     def second_step(self):
         self.arrive()
         scr, r1, r = self.scr, self.rows1, self.rows2
-        whole = None
-        if r < 16:
-            whole = scr["own"][...]
-            for i in range(self.n1 - 1):
-                whole = whole + scr["recv1"][i * r1 : i * r1 + r1].astype(F32)
-        for j in (2, 1, 3, 0):
-            rows = slice(j * r, j * r + r)
-            if r < 16:
-                total = whole[rows]
-            else:
-                total = scr["own"][rows]
-                for i in range(self.n1 - 1):
-                    total = total + scr["recv1"][i * r1 + j * r : i * r1 + j * r + r].astype(F32)
-            if j == 0:
-                scr["own"][rows] = total
-            else:
-                here = pl.ds((j - 1) * r, r)
-                scr["send2"][(j - 1) * r : j * r] = total.astype(scr["send2"].dtype)
-                self.pending.append(
-                    self.copies.send(
-                        scr["send2"].at[here], scr["recv2"].at[here], self.place.shifted(self.second, j)
-                    )
-                )
+        fine = r % 16 == 0
+        for at, count, slots in self.spans:
+            span = slice(at, at + count)
+            if not fine:
+                whole = scr["own"][:, span]
+                for i in slots:
+                    whole = whole + scr["recv1"][i * r1 : i * r1 + r1, span].astype(F32)
+            for j in range(self.n2):
+                rows = slice(j * r, j * r + r)
+                if fine:
+                    total = scr["own"][rows, span]
+                    for i in slots:
+                        total = total + scr["recv1"][i * r1 + j * r : i * r1 + j * r + r, span].astype(F32)
+                else:
+                    total = whole[rows]
+                if j == 0:
+                    scr["own"][rows, span] = total
+                else:
+                    scr["send2"][(j - 1) * r : j * r, span] = total.astype(scr["send2"].dtype)
+        for j in (2, 1, 3):
+            here = pl.ds((j - 1) * r, r)
+            self.pending.append(
+                self.copies.send(scr["send2"].at[here], scr["recv2"].at[here], self.place.shifted(self.second, j))
+            )
 
     def third_step(self):
         self.arrive()
@@ -197,6 +221,7 @@
         own=pltpu.VMEM((r1, width), F32),
         send1=pltpu.VMEM((256 - r1, width), BF16),
         recv1=pltpu.VMEM((256 - r1, width), BF16),
+        relay=pltpu.VMEM((2 * r1, width // 2), BF16),
         send2=pltpu.VMEM((r1 - r2, width), mid),
         recv2=pltpu.VMEM((r1 - r2, width), mid),
         wide3=pltpu.VMEM((2 * n3 * slots, 128), F32),
@@ -208,7 +233,7 @@
 EARLY = (2048, 2048, 512)
 LATE = (768, 768)
 EARLY_OUT = (((0, 16, 16),), ((0, 32, 16),), ((0, 12, 4),))
-LATE_OUT = (((0, 0, 2), (2, 8, 1), (3, 2, 2), (5, 10, 1)), ((0, 4, 2), (2, 9, 1), (3, 6, 2), (5, 11, 1)))
+LATE_OUT = (((0, 0, 2), (2, 8, 1), (3, 2, 1), (4, 10, 1), (5, 3, 1)), ((0, 4, 2), (2, 9, 1), (3, 6, 2), (5, 11, 1)))
 
 
 def greet(place):
@@ -359,7 +384,11 @@
     maps_w[1] = unpack_matrix()
     for part, order in enumerate(ORDERS):
         orders_ref[part] = row_order(place, order)
-    apart = ((iota((144, 144), 0) >= 72) != (iota((144, 144), 1) >= 72)) & (place.lat == 15)
+    lane = iota((144, 576), 1)
+    high = lane < 0
+    for j in range(4):
+        high = high | ((lane >= 144 * j + 72) & (lane < 144 * j + 144))
+    apart = ((iota((144, 576), 0) >= 72) != high) & (place.lat == 15)
     bias[...] = jnp.where(apart, neg_fill, 0.0)
     met()
     halos = []
@@ -423,14 +452,17 @@
     for w in range(2):
         for g in range(4):
             rows, (lq, lk, lv) = group(w, g)
-            scores = dot(head_stack(qkv[rows, lq]), qkv[rows, lk], 1, 1)
-            scores = scores + jnp.concatenate([bias[...]] * 4, axis=0)
-            raised = jnp.exp(scores - jnp.max(scores, axis=-1, keepdims=True))
-            p = raised * (1.0 / jnp.sum(raised, axis=-1, keepdims=True))
+            scores = dot(qkv[rows, lk], head_stack(qkv[rows, lq]), 1, 1) + bias[...]
+            raised = jnp.exp(scores - jnp.max(scores, axis=0, keepdims=True))
+            p = raised * (1.0 / jnp.sum(raised, axis=0, keepdims=True))
             probs[4 * w + g] = p
-            ctx[rows, lq] = head_merge(dot(p.astype(BF16), qkv[rows, lv])).astype(BF16)
+            ctx[rows, lq] = head_merge(dot(p.astype(BF16), qkv[rows, lv], 0, 0)).astype(BF16)
 
     shared_ctx = share(ctx)
+    for copy in halos[1]:
+        copy.wait_recv()
+    cot[OWN] = dot(maps_w[0], arrived[1]).astype(BF16)
+    shared_cot = share(cot)
     loads[3].wait()
     branch = dot(ctx[OWN], wproj[...]).astype(BF16)
     residual = (f32s[X] + branch.astype(F32)).astype(BF16)
@@ -442,10 +474,6 @@
     n2b[OWN] = normed.astype(BF16)
     shared_n2 = share(n2b)
 
-    for copy in halos[1]:
-        copy.wait_recv()
-    cot[OWN] = dot(maps_w[0], arrived[1]).astype(BF16)
-    shared_cot = share(cot)
     loads[4].wait()
     loads[5].wait()
     shared_ff = []
@@ -464,44 +492,54 @@
             copy.wait_recv()
         for part, lhs, rhs in ((0, lhs_n2, gh), (1, lhs_cot, act)):
             early[part].multiply(lhs, rhs, 512 * t, 512 * t, 512)
-            early[part].send_first(512 * t, 512)
-
-    forward_tile(0)
-    forward_tile(1)
+            early[part].send_ring(512 * t, 512)
+
+    for t in range(4):
+        forward_tile(t)
     shared_n2.wait_recv()
+    lhs_n2[...] = dot(orders_ref[0], n2b[...], 1, 1).astype(BF16)
     shared_cot.wait_recv()
-    lhs_n2[...] = dot(orders_ref[0], n2b[...], 1, 1).astype(BF16)
     lhs_cot[...] = dot(orders_ref[1], cot[...], 1, 1).astype(BF16)
     quarter(0)
-    forward_tile(2)
+    shared_ctx.wait_recv()
+    lhs_ctx[...] = dot(orders_ref[2], ctx[...], 1, 1).astype(BF16)
     quarter(1)
-    forward_tile(3)
-    quarter(2)
     grad_n2 = dot(gh[OWN], wfc1[...], 1, 1)
     grad_resid = (cot[OWN].astype(F32) + norm_back(grad_n2, f32s[N2], cols[R2])).astype(BF16)
     gr[OWN] = grad_resid
     shared_gr = share(gr)
+    quarter(2)
+    gctx[...] = dot(gr[OWN], wproj[...], 1, 1).astype(BF16)
     quarter(3)
     block_out = (f32s[X] + dot(act[OWN], wfc2[...])).astype(BF16)
     out_sent = return_home(2, block_out)
-    gctx[...] = dot(gr[OWN], wproj[...], 1, 1).astype(BF16)
-    shared_ctx.wait_recv()
-    lhs_ctx[...] = dot(orders_ref[2], ctx[...], 1, 1).astype(BF16)
+
+    def relay():
+        for part in early[:2]:
+            part.relay()
+
+    relay()
     shared_gr.wait_recv()
     early[2].multiply(lhs_ctx, gr, 0, 0, 512)
     early[2].send_first(0, 512)
-
     shared_n1.wait_recv()
     for i in range(2):
         lhs_n1[i] = dot(orders_ref[i], n1b[...], 1, 1).astype(BF16)
-
-    def late_half(h, shared):
-        for copy in shared:
+    relay()
+
+    pieces = (
+        (((0, 0, 256), (1024, 256, 128)), ((512, 0, 256), (1152, 256, 128))),
+        (((256, 384, 128), (1280, 512, 128)), ((768, 384, 128),)),
+        (((384, 640, 128),), ((896, 512, 128), (1408, 640, 128))),
+    )
+
+    def late_piece(h):
+        for copy in shared_gm[h]:
             copy.wait_recv()
-        for i in range(2):
-            late[i].multiply(lhs_n1.at[i], gm, 512 * i + 256 * h, 384 * h, 256)
-            late[i].multiply(lhs_n1.at[i], gm, 1024 + 256 * h + 128 * i, 384 * h + 256, 128)
-            late[i].send_first(384 * h, 384)
+        for part, moves in zip(late, pieces[h]):
+            for src, at, count in moves:
+                part.multiply(lhs_n1.at[late.index(part)], gm, src, at, count)
+            part.send_first(moves[0][1], sum(count for _, _, count in moves))
 
     shared_gm = []
     for g in range(4):
@@ -509,32 +547,37 @@
             rows, (lq, lk, lv) = group(w, g)
             grad = head_stack(gctx[rows, lq])
             p = probs[4 * w + g]
-            grad_p = dot(grad, qkv[rows, lv], 1, 1)
-            grad_s = (p * (grad_p - jnp.sum(grad_p * p, axis=-1, keepdims=True))).astype(BF16)
-            gm[rows, lv] = dot(p.astype(BF16), grad, 0, 0).astype(BF16)
-            gm[rows, lq] = (head_merge(dot(grad_s, qkv[rows, lk])) * 32 ** (-0.5)).astype(BF16)
-            gm[rows, lk] = dot(grad_s, head_stack(qkv[rows, lq]), 0, 0).astype(BF16)
+            grad_p = dot(qkv[rows, lv], grad, 1, 1)
+            grad_s = (p * (grad_p - jnp.sum(grad_p * p, axis=0, keepdims=True))).astype(BF16)
+            gm[rows, lv] = dot(p.astype(BF16), grad).astype(BF16)
+            gm[rows, lq] = (head_merge(dot(grad_s, qkv[rows, lk], 0, 0)) * 32 ** (-0.5)).astype(BF16)
+            gm[rows, lk] = dot(grad_s, head_stack(qkv[rows, lq])).astype(BF16)
+        if g < 2:
+            relay()
         if g == 1:
             shared_gm.append([share(gm, 512 * j, 256) for j in range(3)])
         if g == 2:
-            late_half(0, shared_gm[0])
+            late_piece(0)
         if g >= 2:
             shared_gm.append([share(gm, 512 * j + 128 * g, 128) for j in range(3)])
 
+    late_piece(1)
     grad_n1 = dot(gm[OWN], wqkv[...], 1, 1).astype(BF16)
-    late_half(1, shared_gm[1] + shared_gm[2])
-    for part in early:
+    late_piece(2)
+    for part in early[:2]:
         part.second_step()
     grad_in = gr[OWN].astype(F32) + norm_back(grad_n1.astype(F32), f32s[N1], cols[R1])
     in_sent = return_home(3, grad_in.astype(BF16))
     out_stored = arrive_home(2, out_sent, out_hbm)
     for part in late:
         part.second_step()
-    for part in early:
+    early[2].second_step()
+    for part in early[:2]:
         part.third_step()
     gin_stored = arrive_home(3, in_sent, gin_hbm)
     for part in late:
         part.third_step()
+    early[2].third_step()
     for part in early:
         part.finish()
     for part in late:
@@ -588,14 +631,14 @@
             pltpu.VMEM((256, both), BF16),
             pltpu.VMEM((256, both), BF16),
             pltpu.VMEM((NT, 3 * D), BF16),
-            pltpu.VMEM((8, 576, 144), F32),
-            pltpu.VMEM((144, 144), F32),
+            pltpu.VMEM((8, 144, 576), F32),
+            pltpu.VMEM((144, 576), F32),
             pltpu.VMEM((NT, D), BF16),
             pltpu.VMEM((3, NT, D), F32),
             pltpu.VMEM((2, NT, 1), F32),
             pltpu.VMEM((4, NT, D), BF16),
-            pltpu.SemaphoreType.DMA((128,)),
-            pltpu.SemaphoreType.DMA((128,)),
+            pltpu.SemaphoreType.DMA((192,)),
+            pltpu.SemaphoreType.DMA((192,)),
             pltpu.SemaphoreType.DMA((8,)),
         ],
         compiler_params=pltpu.CompilerParams(

time: 60.2 us -> 58.8 us (0.977)
  Pallas kernels: 59.5 us -> 57.8 us
    pallas_call x1, Pallas kernels: 57.6 us -> 55.9 us  [on_device(): pl.pallas_call(block_kernel, out_shape=(jax.ShapeDtypeStruct((NT, D), BF1...]
where the time goes in v4:
time: 58.8 us; the launch traced here: 58.5 us
  Pallas kernels  57.8 us (98%)
  between operations  0.64 us (1%)
    pallas_call x1, Pallas kernels, on_device(): pl.pallas_call(block_kernel, out_shape=(jax.ShapeDtypeStruct((NT, D), BF1...  55.9 us
    pallas_call x1, Pallas kernels, on_device(): pl.pallas_call(hand_over, out_shape=tuple((jax.ShapeDtypeStruct(v.shape,...  1.89 us

profile of v4, /device:TPU:8, one launch (start us, length us, event | category | flops | bytes accessed | tf_op | source)
XLA Modules:
  0.0 58.5 jit_solution(18199936958611845351)
XLA Ops:
  0.6 55.9 %shard_map.85 = (bf16[288,512]{1,0:T(8,128)(2,1)}, bf16[288,512]{1,0:T(8,128)(2,1)}, f32[96,128]{1,0:T(8,128)}) custom-call(bf16[288,512]{1,0:T(8,128)(2,1)} %bitcast.4, bf16[288,512]{1,0:T(8,128)(2,1)} %bitcast.5, bf16[512,1536]{1,0:T(8,128)(2,1)} %wqkv_hbm.1, bf16[512,512]{1,0:T(8,128)(2,1)} %wproj_hbm.1, bf16[512,2048]{1,0:T(8,128)(2,1)} %wfc1_hbm.1, ...), custom_call_target="tpu_custom_call" | custom-call | tf_op jit(solution)/shard_map/pallas_call | solution.py:600
  56.6 1.9 %shard_map.86 = (bf16[288,512]{1,0:T(8,128)(2,1)}, bf16[288,512]{1,0:T(8,128)(2,1)}, f32[96,128]{1,0:T(8,128)}) custom-call(bf16[288,512]{1,0:T(8,128)(2,1)} %get-tuple-element.9.refs_0_, bf16[288,512]{1,0:T(8,128)(2,1)} %get-tuple-element.10.refs_1_, f32[96,128]{1,0:T(8,128)} %get-tuple-element.11.refs_2_), custom_call_target="tpu_custom_call" | custom-call | tf_op jit(solution)/shard_map/pallas_call | solution.py:648

commit v5 on v4

--- a/solution.py
+++ b/solution.py
@@ -230,10 +230,10 @@
     )
 
 
-EARLY = (2048, 2048, 512)
-LATE = (768, 768)
-EARLY_OUT = (((0, 16, 16),), ((0, 32, 16),), ((0, 12, 4),))
-LATE_OUT = (((0, 0, 2), (2, 8, 1), (3, 2, 1), (4, 10, 1), (5, 3, 1)), ((0, 4, 2), (2, 9, 1), (3, 6, 2), (5, 11, 1)))
+EARLY = (1536, 2048, 1024)
+LATE = (896, 640)
+EARLY_OUT = (((0, 20, 12),), ((0, 32, 16),), ((0, 16, 4), (4, 12, 4)))
+LATE_OUT = (((0, 0, 2), (2, 8, 1), (3, 2, 1), (4, 10, 1), (5, 3, 1), (6, 11, 1)), ((0, 4, 2), (2, 9, 1), (3, 6, 2)))
 
 
 def greet(place):
@@ -340,7 +340,7 @@
     out_hbm, gin_hbm, wg_ref,
     early, late, orders_ref, wqkv, wproj, wfc1, wfc2,
     packs, arrived, maps_p, maps_w, act, gh, n1b, n2b, cot, ctx, gr, gm,
-    lhs_n1, lhs_n2, lhs_cot, lhs_ctx, qkv, probs, bias, gctx, f32s, cols, ends,
+    lhs_n1, lhs_n2, lhs_n2c, lhs_cot, lhs_ctx, qkv, probs, bias, gctx, f32s, cols, ends,
     send_sems, recv_sems, local_sems,
 ):
     place = Place()
@@ -490,20 +490,26 @@
     def quarter(t):
         for copy in shared_ff[t]:
             copy.wait_recv()
-        for part, lhs, rhs in ((0, lhs_n2, gh), (1, lhs_cot, act)):
-            early[part].multiply(lhs, rhs, 512 * t, 512 * t, 512)
-            early[part].send_ring(512 * t, 512)
+        if t == 0:
+            early[2].multiply(lhs_n2c, gh, 0, 0, 512)
+            early[2].send_first(0, 512)
+        else:
+            early[0].multiply(lhs_n2, gh, 512 * t, 512 * (t - 1), 512)
+            early[0].send_ring(512 * (t - 1), 512)
+        early[1].multiply(lhs_cot, act, 512 * t, 512 * t, 512)
+        early[1].send_ring(512 * t, 512)
 
     for t in range(4):
         forward_tile(t)
     shared_n2.wait_recv()
-    lhs_n2[...] = dot(orders_ref[0], n2b[...], 1, 1).astype(BF16)
+    lhs_n2c[...] = dot(orders_ref[2], n2b[...], 1, 1).astype(BF16)
     shared_cot.wait_recv()
     lhs_cot[...] = dot(orders_ref[1], cot[...], 1, 1).astype(BF16)
     quarter(0)
+    lhs_n2[...] = dot(orders_ref[0], n2b[...], 1, 1).astype(BF16)
+    quarter(1)
     shared_ctx.wait_recv()
     lhs_ctx[...] = dot(orders_ref[2], ctx[...], 1, 1).astype(BF16)
-    quarter(1)
     grad_n2 = dot(gh[OWN], wfc1[...], 1, 1)
     grad_resid = (cot[OWN].astype(F32) + norm_back(grad_n2, f32s[N2], cols[R2])).astype(BF16)
     gr[OWN] = grad_resid
@@ -514,23 +520,24 @@
     block_out = (f32s[X] + dot(act[OWN], wfc2[...])).astype(BF16)
     out_sent = return_home(2, block_out)
 
-    def relay():
-        for part in early[:2]:
-            part.relay()
-
-    relay()
+    def relay(t):
+        if t:
+            early[0].relay()
+        early[1].relay()
+
+    relay(0)
     shared_gr.wait_recv()
-    early[2].multiply(lhs_ctx, gr, 0, 0, 512)
-    early[2].send_first(0, 512)
+    early[2].multiply(lhs_ctx, gr, 0, 512, 512)
+    early[2].send_first(512, 512)
     shared_n1.wait_recv()
     for i in range(2):
         lhs_n1[i] = dot(orders_ref[i], n1b[...], 1, 1).astype(BF16)
-    relay()
+    relay(1)
 
     pieces = (
         (((0, 0, 256), (1024, 256, 128)), ((512, 0, 256), (1152, 256, 128))),
         (((256, 384, 128), (1280, 512, 128)), ((768, 384, 128),)),
-        (((384, 640, 128),), ((896, 512, 128), (1408, 640, 128))),
+        (((384, 640, 128), (1408, 768, 128)), ((896, 512, 128),)),
     )
 
     def late_piece(h):
@@ -553,7 +560,7 @@
             gm[rows, lq] = (head_merge(dot(grad_s, qkv[rows, lk], 0, 0)) * 32 ** (-0.5)).astype(BF16)
             gm[rows, lk] = dot(grad_s, head_stack(qkv[rows, lq])).astype(BF16)
         if g < 2:
-            relay()
+            relay(2 + g)
         if g == 1:
             shared_gm.append([share(gm, 512 * j, 256) for j in range(3)])
         if g == 2:
@@ -578,13 +585,13 @@
     for part in late:
         part.third_step()
     early[2].third_step()
+    copies.drain()
     for part in early:
         part.finish()
     for part in late:
         part.finish()
     out_stored.wait()
     gin_stored.wait()
-    copies.drain()
 
 
 def hand_over(*refs):
@@ -630,6 +637,7 @@
             pltpu.VMEM((256, both), BF16),
             pltpu.VMEM((256, both), BF16),
             pltpu.VMEM((256, both), BF16),
+            pltpu.VMEM((256, both), BF16),
             pltpu.VMEM((NT, 3 * D), BF16),
             pltpu.VMEM((8, 144, 576), F32),
             pltpu.VMEM((144, 576), F32),

time: 58.8 us -> 59.9 us (1.019)
  Pallas kernels: 57.8 us -> 59 us
    pallas_call x1, Pallas kernels: 55.9 us -> 57.1 us  [on_device(): pl.pallas_call(block_kernel, out_shape=(jax.ShapeDtypeStruct((NT, D), BF1...]
where the time goes in v5:
time: 59.9 us; the launch traced here: 59.6 us
  Pallas kernels  59 us (98%)
  between operations  0.64 us (1%)
    pallas_call x1, Pallas kernels, on_device(): pl.pallas_call(block_kernel, out_shape=(jax.ShapeDtypeStruct((NT, D), BF1...  57.1 us
    pallas_call x1, Pallas kernels, on_device(): pl.pallas_call(hand_over, out_shape=tuple((jax.ShapeDtypeStruct(v.shape,...  1.89 us

profile of v5, /device:TPU:8, one launch (start us, length us, event | category | flops | bytes accessed | tf_op | source)
XLA Modules:
  0.0 59.6 jit_solution(1114077087121680176)
XLA Ops:
  0.6 57.1 %shard_map.85 = (bf16[288,512]{1,0:T(8,128)(2,1)}, bf16[288,512]{1,0:T(8,128)(2,1)}, f32[96,128]{1,0:T(8,128)}) custom-call(bf16[288,512]{1,0:T(8,128)(2,1)} %bitcast.4, bf16[288,512]{1,0:T(8,128)(2,1)} %bitcast.5, bf16[512,1536]{1,0:T(8,128)(2,1)} %wqkv_hbm.1, bf16[512,512]{1,0:T(8,128)(2,1)} %wproj_hbm.1, bf16[512,2048]{1,0:T(8,128)(2,1)} %wfc1_hbm.1, ...), custom_call_target="tpu_custom_call" | custom-call | tf_op jit(solution)/shard_map/pallas_call | solution.py:607
  57.7 1.9 %shard_map.86 = (bf16[288,512]{1,0:T(8,128)(2,1)}, bf16[288,512]{1,0:T(8,128)(2,1)}, f32[96,128]{1,0:T(8,128)}) custom-call(bf16[288,512]{1,0:T(8,128)(2,1)} %get-tuple-element.9.refs_0_, bf16[288,512]{1,0:T(8,128)(2,1)} %get-tuple-element.10.refs_1_, f32[96,128]{1,0:T(8,128)} %get-tuple-element.11.refs_2_), custom_call_target="tpu_custom_call" | custom-call | tf_op jit(solution)/shard_map/pallas_call | solution.py:656

commit v6 on v4

--- a/solution.py
+++ b/solution.py
@@ -567,24 +567,24 @@
     for part in early[:2]:
         part.second_step()
     grad_in = gr[OWN].astype(F32) + norm_back(grad_n1.astype(F32), f32s[N1], cols[R1])
-    in_sent = return_home(3, grad_in.astype(BF16))
     out_stored = arrive_home(2, out_sent, out_hbm)
     for part in late:
         part.second_step()
+    in_sent = return_home(3, grad_in.astype(BF16))
     early[2].second_step()
     for part in early[:2]:
         part.third_step()
-    gin_stored = arrive_home(3, in_sent, gin_hbm)
     for part in late:
         part.third_step()
     early[2].third_step()
+    gin_stored = arrive_home(3, in_sent, gin_hbm)
+    copies.drain()
     for part in early:
         part.finish()
     for part in late:
         part.finish()
     out_stored.wait()
     gin_stored.wait()
-    copies.drain()
 
 
 def hand_over(*refs):

time: 58.8 us -> 58 us (0.986)
  Pallas kernels: 57.8 us -> 56.8 us
    pallas_call x1, Pallas kernels: 55.9 us -> 54.9 us  [on_device(): pl.pallas_call(block_kernel, out_shape=(jax.ShapeDtypeStruct((NT, D), BF1...]
where the time goes in v6:
time: 58 us; the launch traced here: 57.5 us
  Pallas kernels  56.8 us (98%)
  between operations  0.64 us (1%)
    pallas_call x1, Pallas kernels, on_device(): pl.pallas_call(block_kernel, out_shape=(jax.ShapeDtypeStruct((NT, D), BF1...  54.9 us
    pallas_call x1, Pallas kernels, on_device(): pl.pallas_call(hand_over, out_shape=tuple((jax.ShapeDtypeStruct(v.shape,...  1.89 us

profile of v6, /device:TPU:8, one launch (start us, length us, event | category | flops | bytes accessed | tf_op | source)
XLA Modules:
  0.0 57.5 jit_solution(13269846830874824595)
XLA Ops:
  0.6 54.9 %shard_map.85 = (bf16[288,512]{1,0:T(8,128)(2,1)}, bf16[288,512]{1,0:T(8,128)(2,1)}, f32[96,128]{1,0:T(8,128)}) custom-call(bf16[288,512]{1,0:T(8,128)(2,1)} %bitcast.4, bf16[288,512]{1,0:T(8,128)(2,1)} %bitcast.5, bf16[512,1536]{1,0:T(8,128)(2,1)} %wqkv_hbm.1, bf16[512,512]{1,0:T(8,128)(2,1)} %wproj_hbm.1, bf16[512,2048]{1,0:T(8,128)(2,1)} %wfc1_hbm.1, ...), custom_call_target="tpu_custom_call" | custom-call | tf_op jit(solution)/shard_map/pallas_call | solution.py:600
  55.6 1.9 %shard_map.86 = (bf16[288,512]{1,0:T(8,128)(2,1)}, bf16[288,512]{1,0:T(8,128)(2,1)}, f32[96,128]{1,0:T(8,128)}) custom-call(bf16[288,512]{1,0:T(8,128)(2,1)} %get-tuple-element.9.refs_0_, bf16[288,512]{1,0:T(8,128)(2,1)} %get-tuple-element.10.refs_1_, f32[96,128]{1,0:T(8,128)} %get-tuple-element.11.refs_2_), custom_call_target="tpu_custom_call" | custom-call | tf_op jit(solution)/shard_map/pallas_call | solution.py:648

commit v7 on v6

--- a/solution.py
+++ b/solution.py
@@ -567,7 +567,6 @@
     for part in early[:2]:
         part.second_step()
     grad_in = gr[OWN].astype(F32) + norm_back(grad_n1.astype(F32), f32s[N1], cols[R1])
-    out_stored = arrive_home(2, out_sent, out_hbm)
     for part in late:
         part.second_step()
     in_sent = return_home(3, grad_in.astype(BF16))
@@ -577,6 +576,7 @@
     for part in late:
         part.third_step()
     early[2].third_step()
+    out_stored = arrive_home(2, out_sent, out_hbm)
     gin_stored = arrive_home(3, in_sent, gin_hbm)
     copies.drain()
     for part in early:

time: 58 us -> 58 us (level)
  no operation moved by 1% of the time
where the time goes in v7:
time: 58 us; the launch traced here: 57.5 us
  Pallas kernels  56.8 us (98%)
  between operations  0.64 us (1%)
    pallas_call x1, Pallas kernels, on_device(): pl.pallas_call(block_kernel, out_shape=(jax.ShapeDtypeStruct((NT, D), BF1...  54.9 us
    pallas_call x1, Pallas kernels, on_device(): pl.pallas_call(hand_over, out_shape=tuple((jax.ShapeDtypeStruct(v.shape,...  1.89 us

profile of v7, /device:TPU:8, one launch (start us, length us, event | category | flops | bytes accessed | tf_op | source)
XLA Modules:
  0.0 57.5 jit_solution(14291003947010950200)
XLA Ops:
  0.6 54.9 %shard_map.85 = (bf16[288,512]{1,0:T(8,128)(2,1)}, bf16[288,512]{1,0:T(8,128)(2,1)}, f32[96,128]{1,0:T(8,128)}) custom-call(bf16[288,512]{1,0:T(8,128)(2,1)} %bitcast.4, bf16[288,512]{1,0:T(8,128)(2,1)} %bitcast.5, bf16[512,1536]{1,0:T(8,128)(2,1)} %wqkv_hbm.1, bf16[512,512]{1,0:T(8,128)(2,1)} %wproj_hbm.1, bf16[512,2048]{1,0:T(8,128)(2,1)} %wfc1_hbm.1, ...), custom_call_target="tpu_custom_call" | custom-call | tf_op jit(solution)/shard_map/pallas_call | solution.py:600
  55.6 1.9 %shard_map.86 = (bf16[288,512]{1,0:T(8,128)(2,1)}, bf16[288,512]{1,0:T(8,128)(2,1)}, f32[96,128]{1,0:T(8,128)}) custom-call(bf16[288,512]{1,0:T(8,128)(2,1)} %get-tuple-element.9.refs_0_, bf16[288,512]{1,0:T(8,128)(2,1)} %get-tuple-element.10.refs_1_, f32[96,128]{1,0:T(8,128)} %get-tuple-element.11.refs_2_), custom_call_target="tpu_custom_call" | custom-call | tf_op jit(solution)/shard_map/pallas_call | solution.py:648
